TPU v7x, 32 devices: a whole 2x2x4 slice. The times are simulated.
32 devices in a mesh: seg: 2 (over x), state: 16 (over z, y, core).
Axes of the slice: x: 2, y: 2, z: 4, core: 2. Of those that a mesh axis runs over, the one named last changes fastest.
Arguments:
- forward_in: float32 [2, 8388608], P('seg', 'state'), may hold values from 0.3 to 28, as said below
- backward_in: float32 [2, 8388608], P('seg', 'state'), may hold values from 0.3 to 28, as said below
- compat_masks: int32 [4, 23], P('seg'), may hold values from 1 to 3
- theta_index: int32 [4, 23], P('seg'), may hold values from 0 to 5
Outputs:
- forward_out: float32 [2, 8388608], P('seg', 'state')
- backward_out: float32 [2, 8388608], P('seg', 'state')
- posterior: float32 [2, 8388608], P('seg', 'state')
- log_scales: float32 [2, 2], P(None, 'seg')
Inputs may be any that keep to these rules, and one draw needn't show every extreme that they name: `compat_masks`: 1 allows anchor 0 only, 2 anchor 1 only, 3 both. `forward_in`: positive. `backward_in`: positive.
All inputs are finite; a program needn't handle non-finite values.
Results may differ from a plain program's by a relative error of at most 0.00011.
Values sent between devices are 32-bit elements; how exact they have to be, the bound alone decides.
A program may use at most 64 MiB of HBM per device.

v0:
```python
import jax
import jax.numpy as jnp
from jax import lax
from jax.sharding import PartitionSpec as P

PENALTY = 0.5
ERROR_RATE = 0.02
BASE_THETA = 0.01


def passed_along(value, axis, steps):
    count = lax.axis_size(axis)
    first, last = (max(0, -steps), min(count, count - steps))
    return lax.ppermute(value, axis, [(source, source + steps) for source in range(first, last)])


def kron_matrix(thetas):
    count = thetas.shape[0]
    width = 2**count
    row_ids = lax.broadcasted_iota(jnp.int32, (width, width), 0)
    col_ids = lax.broadcasted_iota(jnp.int32, (width, width), 1)
    result = jnp.ones((width, width), jnp.float32)
    for which in range(count):
        agrees = row_ids // 2**which % 2 == col_ids // 2**which % 2
        result = result * jnp.where(agrees, 1.0 - thetas[which], thetas[which])
    return result


def mix_local(vector, thetas_local):
    count = thetas_local.shape[0]
    first_bits = min(7, count)
    current = vector.reshape(-1, 2**first_bits)
    current = jnp.dot(
        current,
        kron_matrix(thetas_local[:first_bits]),
        precision=lax.Precision.HIGHEST,
        preferred_element_type=jnp.float32,
    )
    offset = first_bits
    while offset < count:
        width_bits = min(5, count - offset)
        shaped = current.reshape(-1, 2**width_bits, 2**offset)
        current = jnp.einsum(
            "ij,ojk->oik",
            kron_matrix(thetas_local[offset : offset + width_bits]),
            shaped,
            precision=lax.Precision.HIGHEST,
        )
        offset += width_bits
    return current.reshape(-1)


def mix_rows(matrix, thetas_part):
    return jnp.dot(
        kron_matrix(thetas_part),
        matrix,
        precision=lax.Precision.HIGHEST,
        preferred_element_type=jnp.float32,
    )


def anchor_factors(mask_row):
    anchor_zero = jnp.where(mask_row % 2 == 1, 1.0, PENALTY).astype(jnp.float32)
    anchor_one = jnp.where(mask_row // 2 == 1, 1.0, PENALTY).astype(jnp.float32)
    return (anchor_zero, anchor_one)


def bit_product(anchor_zero, anchor_one, first, last):
    product = jnp.ones((1,), jnp.float32)
    for which in range(first, last):
        pair = jnp.stack([anchor_zero[which], anchor_one[which]])
        product = (pair[:, None] * product[None, :]).reshape(-1)
    return product


def emission(mask_row, local_bits, device_index):
    count = mask_row.shape[0]
    anchor_zero, anchor_one = anchor_factors(mask_row)
    product = bit_product(anchor_zero, anchor_one, 0, local_bits)
    high_factor = jnp.ones((), jnp.float32)
    for which in range(count - local_bits):
        anchor = device_index // 2**which % 2
        high_factor = high_factor * jnp.where(
            anchor == 1, anchor_one[local_bits + which], anchor_zero[local_bits + which]
        )
    return ERROR_RATE + (1.0 - ERROR_RATE) * (high_factor * product)


def emission_columns(mask_row, local_bits, high_count, device_index):
    count = mask_row.shape[0]
    anchor_zero, anchor_one = anchor_factors(mask_row)
    low_bits = local_bits - high_count
    low_part = bit_product(anchor_zero, anchor_one, 0, low_bits)
    own_factor = jnp.ones((), jnp.float32)
    for which in range(high_count):
        anchor = device_index // 2**which % 2
        own_factor = own_factor * jnp.where(
            anchor == 1, anchor_one[low_bits + which], anchor_zero[low_bits + which]
        )
    high_part = bit_product(anchor_zero, anchor_one, local_bits, count)
    table = high_part[:, None] * own_factor * low_part[None, :]
    return ERROR_RATE + (1.0 - ERROR_RATE) * table.reshape(-1)


def shards(forward_in, backward_in, compat_masks, theta_index):
    groups = lax.axis_size("state")
    high_count = groups.bit_length() - 1
    device_index = lax.axis_index("state")
    initial = forward_in[0]
    forward = initial
    backward = backward_in[0]
    local_size = initial.shape[0]
    local_bits = local_size.bit_length() - 1
    low_bits = local_bits - high_count
    total_states = local_size * groups
    thetas = BASE_THETA * 2.0 ** theta_index.astype(jnp.float32)
    markers = compat_masks.shape[0]
    emissions = [
        emission(compat_masks[marker], local_bits, device_index) for marker in range(markers)
    ]
    log_fwd = jnp.zeros((), jnp.float32)
    log_bwd = jnp.zeros((), jnp.float32)
    col_emissions = [
        emission_columns(compat_masks[marker], local_bits, high_count, device_index)
        for marker in range(markers)
    ]
    for marker in range(markers):
        behind = markers - 1 - marker
        if marker % 2 == 0:
            fwd_part = mix_local(forward, thetas[marker][:local_bits]).reshape(groups, -1)
            bwd_part = mix_local(emissions[behind] * backward, thetas[behind][:local_bits]).reshape(
                groups, -1
            )
            fwd_part, bwd_part = (
                lax.all_to_all(fwd_part, "state", split_axis=0, concat_axis=0, tiled=True),
                lax.all_to_all(bwd_part, "state", split_axis=0, concat_axis=0, tiled=True),
            )
            fwd_part = mix_rows(fwd_part, thetas[marker][local_bits:])
            bwd_part = mix_rows(bwd_part, thetas[behind][local_bits:])
            forward = col_emissions[marker] * fwd_part.reshape(-1)
            backward = bwd_part.reshape(-1)
        else:
            fwd_part = mix_local(forward, thetas[marker][:low_bits]).reshape(groups, -1)
            bwd_part = mix_local(
                col_emissions[behind] * backward, thetas[behind][:low_bits]
            ).reshape(groups, -1)
            fwd_part = mix_rows(fwd_part, thetas[marker][local_bits:])
            bwd_part = mix_rows(bwd_part, thetas[behind][local_bits:])
            fwd_part, bwd_part = (
                lax.all_to_all(fwd_part, "state", split_axis=0, concat_axis=0, tiled=True),
                lax.all_to_all(bwd_part, "state", split_axis=0, concat_axis=0, tiled=True),
            )
            fwd_part = mix_rows(fwd_part, thetas[marker][low_bits:local_bits])
            bwd_part = mix_rows(bwd_part, thetas[behind][low_bits:local_bits])
            forward = emissions[marker] * fwd_part.reshape(-1)
            backward = bwd_part.reshape(-1)
        totals = lax.psum((jnp.sum(forward), jnp.sum(backward)), "state")
        mean_fwd = totals[0] / total_states
        mean_bwd = totals[1] / total_states
        forward = forward / mean_fwd
        backward = backward / mean_bwd
        log_fwd = log_fwd + jnp.log(mean_fwd)
        log_bwd = log_bwd + jnp.log(mean_bwd)
    received = passed_along(forward, "seg", 1)
    left_side = jnp.where(lax.axis_index("seg") == 0, initial, received)
    product = left_side * backward
    post_total = lax.psum(jnp.sum(product), "state")
    posterior = product / (post_total / total_states)
    log_scales = jnp.stack([log_fwd, log_bwd]).reshape(2, 1)
    return (forward[None, :], backward[None, :], posterior[None, :], log_scales)


def solution(mesh):
    placed = (P("seg", "state"), P("seg", "state"), P("seg", None), P("seg", None))
    return jax.shard_map(
        shards,
        mesh=mesh,
        in_specs=placed,
        out_specs=(P("seg", "state"), P("seg", "state"), P("seg", "state"), P(None, "seg")),
        check_vma=False,
    )
```

profile of v0, /device:TPU:0, one launch (start us, length us, event | category | flops | bytes accessed | tf_op | source)
XLA Modules:
  0.0 542.9 jit_solution(16074583059732831398)
XLA Ops:
  9.1 2.7 pad_maximum_fusion.16
  18.0 2.7 pad_maximum_fusion.10
  26.2 2.7 pad_maximum_fusion.4
  48.4 6.6 %fusion.51 = f32[128,32,128]{2,1,0:T(8,128)S(1)} fusion(f32[128,32,128]{2,1,0:T(8,128)S(1)} %fusion.15, f32[]{:T(128)} %bitcast.69, f32[]{:T(128)S(6)} %sub.765, f32[]{:T(128)} %bitcast.68, f32[]{:T(128)S(6)} %sub.764, f32[]{:T(128)} %bitcast.67, f32[]{:T(128)S(6)} %sub.763, f32[]{:T(128)} %bitcast.66, f32[]{:T(128)S(6)} %sub.762, f32[]{:T(128)} %bitcast.65, ...), kind=kOutput, calls=%fused_computation.145 | convolution fusion | flops 808189952 | bytes 4201272 | tf_op jit(solution)/shard_map/dot_general | solution.py:33
  55.0 6.4 %convolution_bitcast_fusion.8 = f32[128,32,128]{2,1,0:T(8,128)} fusion(f32[128,32,128]{2,1,0:T(8,128)S(1)} %fusion.51, f32[]{:T(128)} %bitcast.75, f32[]{:T(128)S(6)} %sub.770, f32[]{:T(128)} %bitcast.74, f32[]{:T(128)S(6)} %sub.769, f32[]{:T(128)} %bitcast.73, f32[]{:T(128)S(6)} %sub.768, f32[]{:T(128)} %bitcast.72, f32[]{:T(128)S(6)} %sub.767, ...), kind=kOutput, calls=%fused_computation.42 | convolution fusion | flops 201451520 | bytes 4195496 | tf_op jit(solution)/shard_map/ij,ojk->oik/dot_general | solution.py:43
  66.8 5.2 convolution_bitcast_fusion.4
  74.6 6.1 %convolution_bitcast_fusion = f32[1,4,131072]{2,1,0:T(4,128)} fusion(f32[4,131072]{1,0:T(4,128)S(1)} %bitcast.338, f32[]{:T(128)} %bitcast.13, f32[]{:T(128)S(6)} %sub.719, f32[]{:T(128)} %bitcast.12, f32[]{:T(128)S(6)} %sub.717, s32[4]{0:T(128)S(1)} %get-tuple-element.232, s32[4]{0:T(128)S(1)} %get-tuple-element.233, pred[4]{0:T(512)(128)(4,1)S(1)} %compare_and_fusion.2), kind=kOutput, calls=%fused_computation | convolution fusion | flops 25166480 | bytes 4194356 | tf_op jit(solution)/shard_map/ij,ojk->oik/dot_general | solution.py:43
  80.7 5.8 %all_to_all.45 = f32[16,1,32768]{2,1,0:T(1,128)} reshape(f32[1,4,131072]{2,1,0:T(4,128)} %convolution_bitcast_fusion) | data formatting | bytes 4194304 | tf_op jit(solution)/shard_map/all_to_all | solution.py:136
  86.5 7.8 %all-to-all-start.2 = ((f32[16,1,32768]{2,1,0:T(1,128)}), f32[16,1,32768]{2,1,0:T(1,128)}, u32[]{:S(2)}, u32[]{:S(2)}) async-start(f32[16,1,32768]{2,1,0:T(1,128)} %all_to_all.45), calls=%async_computation.2 | async-start | bytes 4194304 | tf_op jit(solution)/shard_map/all_to_all | solution.py:136
  103.5 7.9 %convolution_bitcast_fusion.6 = f32[4096,128]{0,1:T(8,128)} fusion(f32[4096,128]{1,0:T(8,128)S(1)} %bitcast.325, f32[]{:T(128)} %bitcast.41, f32[]{:T(128)S(6)} %sub.741, f32[]{:T(128)} %bitcast.40, f32[]{:T(128)S(6)} %sub.739, f32[]{:T(128)} %bitcast.39, f32[]{:T(128)S(6)} %sub.737, f32[]{:T(128)} %bitcast.38, f32[]{:T(128)S(6)} %sub.735, f32[]{:T(128)} %bitcast.37, ...), kind=kOutput, calls=%fused_computation.6 | convolution fusion | flops 808189952 | bytes 4201272 | tf_op jit(solution)/shard_map/dot_general | solution.py:33
  116.5 6.4 %convolution_bitcast_fusion.10 = f32[128,32,128]{2,1,0:T(8,128)} fusion(f32[128,32,128]{2,1,0:T(8,128)S(1)} %bitcast.334, f32[]{:T(128)} %bitcast.49, f32[]{:T(128)S(6)} %sub.750, f32[]{:T(128)} %bitcast.48, f32[]{:T(128)S(6)} %sub.748, f32[]{:T(128)} %bitcast.47, f32[]{:T(128)S(6)} %sub.746, f32[]{:T(128)} %bitcast.46, f32[]{:T(128)S(6)} %sub.744, ...), kind=kOutput, calls=%fused_computation.44 | convolution fusion | flops 201451520 | bytes 4195496 | tf_op jit(solution)/shard_map/ij,ojk->oik/dot_general | solution.py:43
  128.0 5.2 convolution_bitcast_fusion.5
  135.8 6.5 %convolution_bitcast_fusion.1 = f32[1,4,131072]{2,1,0:T(4,128)} fusion(f32[4,131072]{1,0:T(4,128)S(1)} %bitcast.337, f32[]{:T(128)} %bitcast.60, f32[]{:T(128)S(6)} %sub.758, f32[]{:T(128)} %bitcast.59, f32[]{:T(128)S(6)} %sub.756, s32[4]{0:T(128)S(1)} %get-tuple-element.232, s32[4]{0:T(128)S(1)} %get-tuple-element.233, pred[4]{0:T(512)(128)(4,1)S(1)} %compare_and_fusion.2), kind=kOutput, calls=%fused_computation.1 | convolution fusion | flops 25166480 | bytes 4194356 | tf_op jit(solution)/shard_map/ij,ojk->oik/dot_general | solution.py:43
  142.3 5.8 %all_to_all.44 = f32[16,1,32768]{2,1,0:T(1,128)} reshape(f32[1,4,131072]{2,1,0:T(4,128)} %convolution_bitcast_fusion.1) | data formatting | bytes 4194304 | tf_op jit(solution)/shard_map/all_to_all | solution.py:135
  171.3 6.1 %all-to-all-start = ((f32[16,1,32768]{2,1,0:T(1,128)}), f32[16,1,32768]{2,1,0:T(1,128)S(1)}, u32[]{:S(2)}, u32[]{:S(2)}) async-start(f32[16,1,32768]{2,1,0:T(1,128)} %all_to_all.44), calls=%async_computation | async-start | bytes 4194304 | tf_op jit(solution)/shard_map/all_to_all | solution.py:135
  195.3 8.9 %fusion.391 = (f32[]{:T(128)}, f32[16,32768]{1,0:T(8,128)}) fusion(f32[16,1,32768]{2,1,0:T(1,128)} %all-to-all-done.2, f32[]{:T(128)} %bitcast.17, f32[]{:T(128)S(6)} %sub.723, f32[]{:T(128)} %bitcast.16, f32[]{:T(128)S(6)} %sub.722, f32[]{:T(128)} %bitcast.15, f32[]{:T(128)S(6)} %sub.721, f32[]{:T(128)} %bitcast.14, f32[]{:T(128)S(6)} %sub.720, ...), kind=kOutput, calls=%fused_computation.708 | convolution fusion | flops 101211904 | bytes 4194772 | tf_op jit(solution)/shard_map/dot_general | solution.py:54
  204.3 14.3 %all-to-all-done = f32[16,1,32768]{2,1,0:T(1,128)S(1)} async-done(((f32[16,1,32768]{2,1,0:T(1,128)}), f32[16,1,32768]{2,1,0:T(1,128)S(1)}, u32[]{:S(2)}, u32[]{:S(2)}) %all-to-all-start) | async-done | bytes 2097184 | tf_op jit(solution)/shard_map/all_to_all | solution.py:135
  218.5 7.4 %multiply_reduce_fusion = (f32[]{:T(128)}, f32[16,32768]{1,0:T(8,128)}) fusion(f32[32768]{0:T(1024)S(1)} %bitcast.345, f32[16]{0:T(128)S(1)} %copy-done.92, f32[16,1,32768]{2,1,0:T(1,128)S(1)} %all-to-all-done, f32[]{:T(128)} %bitcast.34, f32[]{:T(128)S(6)} %sub.728, f32[]{:T(128)} %bitcast.33, f32[]{:T(128)S(6)} %sub.727, f32[]{:T(128)} %bitcast.32, ...), kind=kOutput, calls=%fused_computation.39 | convolution fusion | flops 103309056 | bytes 4325908 | tf_op jit(solution)/shard_map/dot_general | solution.py:54
  226.0 40.1 %all-reduce.1 = (f32[]{:T(128)}, f32[]{:T(128)}) all-reduce(f32[]{:T(128)} %get-tuple-element.168, f32[]{:T(128)} %get-tuple-element.170), channel_id=1, replica_groups=mesh['seg'=2,'state'=16] {'state'}, use_global_device_ids=true, to_apply=%region_1.2 | all-reduce | flops 2 | bytes 16 | tf_op jit(solution)/shard_map/psum | solution.py:157
  266.7 3.1 broadcast_divide_fusion.2
  269.8 2.8 div.697
  274.9 2.7 fusion.23
  277.9 6.6 %fusion.49 = f32[128,32,128]{2,1,0:T(8,128)S(1)} fusion(f32[128,32,128]{2,1,0:T(8,128)S(1)} %get-tuple-element.18, f32[]{:T(128)} %bitcast.41, f32[]{:T(128)S(6)} %sub.741, f32[]{:T(128)} %bitcast.40, f32[]{:T(128)S(6)} %sub.739, f32[]{:T(128)} %bitcast.39, f32[]{:T(128)S(6)} %sub.737, f32[]{:T(128)} %bitcast.38, f32[]{:T(128)S(6)} %sub.735, f32[]{:T(128)} %bitcast.37, ...), kind=kOutput, calls=%fused_computation.143 | convolution fusion | flops 808189952 | bytes 4201272 | tf_op jit(solution)/shard_map/dot_general | solution.py:33
  284.6 6.4 %convolution_bitcast_fusion.7 = f32[128,32,128]{2,1,0:T(8,128)} fusion(f32[128,32,128]{2,1,0:T(8,128)S(1)} %fusion.49, f32[]{:T(128)} %bitcast.49, f32[]{:T(128)S(6)} %sub.750, f32[]{:T(128)} %bitcast.48, f32[]{:T(128)S(6)} %sub.748, f32[]{:T(128)} %bitcast.47, f32[]{:T(128)S(6)} %sub.746, f32[]{:T(128)} %bitcast.46, f32[]{:T(128)S(6)} %sub.744, ...), kind=kOutput, calls=%fused_computation.41 | convolution fusion | flops 201451520 | bytes 4195496 | tf_op jit(solution)/shard_map/ij,ojk->oik/dot_general | solution.py:43
  291.0 2.7 reshape.938
  293.8 5.5 %fusion.163 = f32[16,4096,8]{1,2,0:T(8,128)S(1)} fusion(f32[16,8,4096]{2,1,0:T(8,128)} %reshape.938, f32[]{:T(128)} %bitcast.54, f32[]{:T(128)S(6)} %sub.753, f32[]{:T(128)} %bitcast.53, f32[]{:T(128)S(6)} %sub.752, f32[]{:T(128)} %bitcast.52, f32[]{:T(128)S(6)} %sub.751, s32[8]{0:T(128)S(1)} %get-tuple-element.261, s32[8]{0:T(128)S(1)} %get-tuple-element.262, ...), kind=kOutput, calls=%fused_computation.376 | convolution fusion | flops 50336000 | bytes 4194472 | tf_op jit(solution)/shard_map/ij,ojk->oik/dot_general | solution.py:43
  300.6 4.4 convolution_bitcast_fusion.2
  305.0 3.5 copy.14
  308.5 4.6 all-to-all-start.3
  316.2 6.6 %fusion.53 = f32[128,32,128]{2,1,0:T(8,128)S(1)} fusion(f32[128,32,128]{2,1,0:T(8,128)S(1)} %get-tuple-element.19, f32[]{:T(128)} %bitcast.69, f32[]{:T(128)S(6)} %sub.765, f32[]{:T(128)} %bitcast.68, f32[]{:T(128)S(6)} %sub.764, f32[]{:T(128)} %bitcast.67, f32[]{:T(128)S(6)} %sub.763, f32[]{:T(128)} %bitcast.66, f32[]{:T(128)S(6)} %sub.762, f32[]{:T(128)} %bitcast.65, ...), kind=kOutput, calls=%fused_computation.147 | convolution fusion | flops 808189952 | bytes 4201272 | tf_op jit(solution)/shard_map/dot_general | solution.py:33
  322.8 5.0 convolution_bitcast_fusion.9
  329.9 5.5 %fusion.165 = f32[16,4096,8]{1,2,0:T(8,128)S(1)} fusion(f32[16,8,4096]{2,1,0:T(8,128)} %reshape.934, f32[]{:T(128)} %bitcast.80, f32[]{:T(128)S(6)} %sub.775, f32[]{:T(128)} %bitcast.79, f32[]{:T(128)S(6)} %sub.773, f32[]{:T(128)} %bitcast.78, f32[]{:T(128)S(6)} %sub.771, s32[8]{0:T(128)S(1)} %copy-done.85, s32[8]{0:T(128)S(1)} %copy-done.87, ...), kind=kOutput, calls=%fused_computation.378 | convolution fusion | flops 50336000 | bytes 4194472 | tf_op jit(solution)/shard_map/ij,ojk->oik/dot_general | solution.py:43
  336.8 4.5 convolution_bitcast_fusion.3
  341.3 3.5 copy.12
  344.8 9.5 %all-to-all-done.3 = f32[16,1,32768]{2,1,0:T(1,128)} async-done(((f32[16,1,32768]{2,1,0:T(1,128)}), f32[16,1,32768]{2,1,0:T(1,128)}, u32[]{:S(2)}, u32[]{:S(2)}) %all-to-all-start.3) | async-done | bytes 2097184 | tf_op jit(solution)/shard_map/all_to_all | solution.py:151
  354.3 11.4 %all-to-all-start.1 = ((f32[16,1,32768]{2,1,0:T(1,128)}), f32[16,1,32768]{2,1,0:T(1,128)}, u32[]{:S(2)}, u32[]{:S(2)}) async-start(f32[16,1,32768]{2,1,0:T(1,128)} %copy.12), calls=%async_computation.1 | async-start | bytes 4194304 | tf_op jit(solution)/shard_map/all_to_all | solution.py:150
  371.3 6.2 %copy.29 = f32[1,1,2,262144]{3,1,2,0:T(1,128)} copy(f32[1,1,2,262144]{3,2,1,0:T(2,128)S(1)} %get-tuple-element.17) | data formatting | bytes 4194304
  377.6 9.0 %fusion.392 = (f32[]{:T(128)}, f32[16,32768]{1,0:T(8,128)}) fusion(f32[16,1,32768]{2,1,0:T(1,128)} %all-to-all-done.3, f32[]{:T(128)} %bitcast.60, f32[]{:T(128)S(6)} %sub.758, f32[]{:T(128)} %bitcast.59, f32[]{:T(128)S(6)} %sub.756, f32[]{:T(128)} %bitcast.56, f32[]{:T(128)S(6)} %sub.755, f32[]{:T(128)} %bitcast.55, f32[]{:T(128)S(6)} %sub.754, ...), kind=kOutput, calls=%fused_computation.709 | convolution fusion | flops 101211904 | bytes 4194772 | tf_op jit(solution)/shard_map/dot_general | solution.py:54
  386.6 20.2 %all-to-all-done.1 = f32[16,1,32768]{2,1,0:T(1,128)} async-done(((f32[16,1,32768]{2,1,0:T(1,128)}), f32[16,1,32768]{2,1,0:T(1,128)}, u32[]{:S(2)}, u32[]{:S(2)}) %all-to-all-start.1) | async-done | bytes 2097184 | tf_op jit(solution)/shard_map/all_to_all | solution.py:150
  406.8 7.8 %fusion.20 = (f32[]{:T(128)}, f32[16,32768]{1,0:T(8,128)S(1)}) fusion(f32[8,32768]{1,0:T(8,128)S(1)} %copy-done.6, f32[16]{0:T(128)S(1)} %mul.1376, f32[]{:T(128)S(6)} %mul.1158, f32[16,1,32768]{2,1,0:T(1,128)} %all-to-all-done.1, f32[]{:T(128)} %bitcast.13, f32[]{:T(128)S(6)} %sub.719, f32[]{:T(128)} %bitcast.12, f32[]{:T(128)S(6)} %sub.717, f32[]{:T(128)} %bitcast.11, ...), kind=kOutput, calls=%fused_computation.29 | convolution fusion | flops 103833344 | bytes 5243416 | tf_op jit(solution)/shard_map/dot_general | solution.py:54
  414.6 39.8 %all-reduce = (f32[]{:T(128)}, f32[]{:T(128)}) all-reduce(f32[]{:T(128)} %get-tuple-element.172, f32[]{:T(128)} %get-tuple-element.174), channel_id=1, replica_groups=mesh['seg'=2,'state'=16] {'state'}, use_global_device_ids=true, to_apply=%region_3.4 | all-reduce | flops 2 | bytes 16 | tf_op jit(solution)/shard_map/psum | solution.py:157
  458.3 4.9 collective-permute-start
  465.4 3.3 multiply_divide_fusion.1
  471.4 3.5 copy.42
  475.4 27.2 %collective-permute-done = f32[524288]{0:T(1024)} collective-permute-done((f32[524288]{0:T(1024)}, f32[524288]{0:T(1024)}, u32[]{:S(2)}, u32[]{:S(2)}) %collective-permute-start) | collective-permute-done | bytes 2097184 | tf_op jit(solution)/shard_map/ppermute | solution.py:14
  502.7 4.0 fusion.379
  506.7 32.3 %psum.39 = f32[]{:T(128)} all-reduce(f32[]{:T(128)} %get-tuple-element.8), channel_id=1, replica_groups=mesh['seg'=2,'state'=16] {'state'}, use_global_device_ids=true, to_apply=%region_9.10 | all-reduce | flops 1 | bytes 8 | tf_op jit(solution)/shard_map/psum | solution.py:167
  539.6 3.1 broadcast_divide_fusion
  (374 shorter events, 93.4 us)
Async XLA Ops:
  0.7 102.6 %copy-start.42 = (pred[128]{0:T(512)(128)(4,1)}, pred[128]{0:T(512)(128)(4,1)S(1)}, u32[]{:S(2)}) copy-start(pred[128]{0:T(512)(128)(4,1)S(1)} %get-tuple-element.202) | copy-start | bytes 388
  0.7 102.6 %copy-start.44 = (pred[128]{0:T(512)(128)(4,1)}, pred[128]{0:T(512)(128)(4,1)S(1)}, u32[]{:S(2)}) copy-start(pred[128]{0:T(512)(128)(4,1)S(1)} %get-tuple-element.203) | copy-start | bytes 388
  0.7 102.6 %copy-start.46 = (pred[128]{0:T(512)(128)(4,1)}, pred[128]{0:T(512)(128)(4,1)S(1)}, u32[]{:S(2)}) copy-start(pred[128]{0:T(512)(128)(4,1)S(1)} %get-tuple-element.204) | copy-start | bytes 388
  0.8 102.6 %copy-start.48 = (pred[128]{0:T(512)(128)(4,1)}, pred[128]{0:T(512)(128)(4,1)S(1)}, u32[]{:S(2)}) copy-start(pred[128]{0:T(512)(128)(4,1)S(1)} %get-tuple-element.205) | copy-start | bytes 388
  0.8 102.6 %copy-start.50 = (pred[128]{0:T(512)(128)(4,1)}, pred[128]{0:T(512)(128)(4,1)S(1)}, u32[]{:S(2)}) copy-start(pred[128]{0:T(512)(128)(4,1)S(1)} %get-tuple-element.206) | copy-start | bytes 388
  0.8 102.6 %copy-start.52 = (pred[128]{0:T(512)(128)(4,1)}, pred[128]{0:T(512)(128)(4,1)S(1)}, u32[]{:S(2)}) copy-start(pred[128]{0:T(512)(128)(4,1)S(1)} %get-tuple-element.207) | copy-start | bytes 388
  0.8 102.6 %copy-start.54 = (s32[128]{0:T(128)}, s32[128]{0:T(128)S(1)}, u32[]{:S(2)}) copy-start(s32[128]{0:T(128)S(1)} %get-tuple-element.208) | copy-start | bytes 1540
  0.8 102.6 %copy-start.56 = (s32[128]{0:T(128)}, s32[128]{0:T(128)S(1)}, u32[]{:S(2)}) copy-start(s32[128]{0:T(128)S(1)} %get-tuple-element.209) | copy-start | bytes 1540
  0.8 102.6 %copy-start.58 = (s32[128]{0:T(128)}, s32[128]{0:T(128)S(1)}, u32[]{:S(2)}) copy-start(s32[128]{0:T(128)S(1)} %get-tuple-element.210) | copy-start | bytes 1540
  0.9 102.6 %copy-start.60 = (s32[128]{0:T(128)}, s32[128]{0:T(128)S(1)}, u32[]{:S(2)}) copy-start(s32[128]{0:T(128)S(1)} %get-tuple-element.211) | copy-start | bytes 1540
  0.9 102.6 %copy-start.62 = (s32[128]{0:T(128)}, s32[128]{0:T(128)S(1)}, u32[]{:S(2)}) copy-start(s32[128]{0:T(128)S(1)} %get-tuple-element.212) | copy-start | bytes 1540
  0.9 102.6 %copy-start.64 = (s32[128]{0:T(128)}, s32[128]{0:T(128)S(1)}, u32[]{:S(2)}) copy-start(s32[128]{0:T(128)S(1)} %get-tuple-element.213) | copy-start | bytes 1540
  0.9 102.6 %copy-start.66 = (s32[128]{0:T(128)}, s32[128]{0:T(128)S(1)}, u32[]{:S(2)}) copy-start(s32[128]{0:T(128)S(1)} %get-tuple-element.214) | copy-start | bytes 1540
  0.9 102.6 %copy-start.68 = (s32[128]{0:T(128)}, s32[128]{0:T(128)S(1)}, u32[]{:S(2)}) copy-start(s32[128]{0:T(128)S(1)} %get-tuple-element.215) | copy-start | bytes 1540
  0.9 102.6 %copy-start.70 = (s32[128]{0:T(128)}, s32[128]{0:T(128)S(1)}, u32[]{:S(2)}) copy-start(s32[128]{0:T(128)S(1)} %get-tuple-element.216) | copy-start | bytes 1540
  0.9 102.6 %copy-start.72 = (s32[128]{0:T(128)}, s32[128]{0:T(128)S(1)}, u32[]{:S(2)}) copy-start(s32[128]{0:T(128)S(1)} %get-tuple-element.217) | copy-start | bytes 1540
  1.0 102.5 %copy-start.74 = (s32[128]{0:T(128)}, s32[128]{0:T(128)S(1)}, u32[]{:S(2)}) copy-start(s32[128]{0:T(128)S(1)} %get-tuple-element.218) | copy-start | bytes 1540
  1.0 102.5 %copy-start.76 = (s32[128]{0:T(128)}, s32[128]{0:T(128)S(1)}, u32[]{:S(2)}) copy-start(s32[128]{0:T(128)S(1)} %get-tuple-element.219) | copy-start | bytes 1540
  1.0 126.9 %copy-start.8 = (s32[32]{0:T(128)}, s32[32]{0:T(128)S(1)}, u32[]{:S(2)}) copy-start(s32[32]{0:T(128)S(1)} %get-tuple-element.224) | copy-start | bytes 388
  1.0 126.9 %copy-start.10 = (s32[32]{0:T(128)}, s32[32]{0:T(128)S(1)}, u32[]{:S(2)}) copy-start(s32[32]{0:T(128)S(1)} %get-tuple-element.225) | copy-start | bytes 388
  1.1 126.9 %copy-start.12 = (s32[32]{0:T(128)}, s32[32]{0:T(128)S(1)}, u32[]{:S(2)}) copy-start(s32[32]{0:T(128)S(1)} %get-tuple-element.226) | copy-start | bytes 388
  1.1 126.9 %copy-start.14 = (s32[32]{0:T(128)}, s32[32]{0:T(128)S(1)}, u32[]{:S(2)}) copy-start(s32[32]{0:T(128)S(1)} %get-tuple-element.227) | copy-start | bytes 388
  1.1 126.9 %copy-start.16 = (s32[32]{0:T(128)}, s32[32]{0:T(128)S(1)}, u32[]{:S(2)}) copy-start(s32[32]{0:T(128)S(1)} %get-tuple-element.228) | copy-start | bytes 388
  1.1 126.9 %copy-start.18 = (s32[32]{0:T(128)}, s32[32]{0:T(128)S(1)}, u32[]{:S(2)}) copy-start(s32[32]{0:T(128)S(1)} %get-tuple-element.229) | copy-start | bytes 388
  1.1 126.9 %copy-start.20 = (s32[32]{0:T(128)}, s32[32]{0:T(128)S(1)}, u32[]{:S(2)}) copy-start(s32[32]{0:T(128)S(1)} %get-tuple-element.230) | copy-start | bytes 388
  1.1 126.9 %copy-start.22 = (s32[32]{0:T(128)}, s32[32]{0:T(128)S(1)}, u32[]{:S(2)}) copy-start(s32[32]{0:T(128)S(1)} %get-tuple-element.231) | copy-start | bytes 388
  4.0 43.8 %copy-start.7 = (f32[1,524288]{1,0:T(1,128)S(1)}, f32[1,524288]{1,0:T(1,128)}, u32[]{:S(2)}) copy-start(f32[1,524288]{1,0:T(1,128)} %param.5) | copy-start | bytes 6291460
  86.5 84.8 %all-to-all-start.2 = ((f32[16,1,32768]{2,1,0:T(1,128)}), f32[16,1,32768]{2,1,0:T(1,128)}, u32[]{:S(2)}, u32[]{:S(2)}) async-start(f32[16,1,32768]{2,1,0:T(1,128)} %all_to_all.45), calls=%async_computation.2 | async-start | bytes 4194304 | tf_op jit(solution)/shard_map/all_to_all | solution.py:136
  171.3 47.2 %all-to-all-start = ((f32[16,1,32768]{2,1,0:T(1,128)}), f32[16,1,32768]{2,1,0:T(1,128)S(1)}, u32[]{:S(2)}, u32[]{:S(2)}) async-start(f32[16,1,32768]{2,1,0:T(1,128)} %all_to_all.44), calls=%async_computation | async-start | bytes 4194304 | tf_op jit(solution)/shard_map/all_to_all | solution.py:135
  195.1 105.5 %copy-start.24 = (pred[16]{0:T(512)(128)(4,1)}, pred[16]{0:T(512)(128)(4,1)S(1)}, u32[]{:S(2)}) copy-start(pred[16]{0:T(512)(128)(4,1)S(1)} %compare_and_fusion.15) | copy-start | bytes 52
  195.1 105.4 %copy-start.26 = (pred[16]{0:T(512)(128)(4,1)}, pred[16]{0:T(512)(128)(4,1)S(1)}, u32[]{:S(2)}) copy-start(pred[16]{0:T(512)(128)(4,1)S(1)} %get-tuple-element.234) | copy-start | bytes 52
  195.1 105.4 %copy-start.28 = (pred[16]{0:T(512)(128)(4,1)}, pred[16]{0:T(512)(128)(4,1)S(1)}, u32[]{:S(2)}) copy-start(pred[16]{0:T(512)(128)(4,1)S(1)} %get-tuple-element.235) | copy-start | bytes 52
  195.1 105.4 %copy-start.30 = (s32[16]{0:T(128)}, s32[16]{0:T(128)S(1)}, u32[]{:S(2)}) copy-start(s32[16]{0:T(128)S(1)} %get-tuple-element.236) | copy-start | bytes 196
  195.1 105.4 %copy-start.32 = (s32[16]{0:T(128)}, s32[16]{0:T(128)S(1)}, u32[]{:S(2)}) copy-start(s32[16]{0:T(128)S(1)} %get-tuple-element.237) | copy-start | bytes 196
  195.2 105.4 %copy-start.34 = (s32[16]{0:T(128)}, s32[16]{0:T(128)S(1)}, u32[]{:S(2)}) copy-start(s32[16]{0:T(128)S(1)} %get-tuple-element.238) | copy-start | bytes 196
  195.2 105.4 %copy-start.36 = (s32[16]{0:T(128)}, s32[16]{0:T(128)S(1)}, u32[]{:S(2)}) copy-start(s32[16]{0:T(128)S(1)} %get-tuple-element.239) | copy-start | bytes 196
  195.2 105.4 %copy-start.38 = (s32[16]{0:T(128)}, s32[16]{0:T(128)S(1)}, u32[]{:S(2)}) copy-start(s32[16]{0:T(128)S(1)} %get-tuple-element.240) | copy-start | bytes 196
  195.2 105.4 %copy-start.40 = (s32[16]{0:T(128)}, s32[16]{0:T(128)S(1)}, u32[]{:S(2)}) copy-start(s32[16]{0:T(128)S(1)} %get-tuple-element.241) | copy-start | bytes 196
  195.2 98.5 %copy-start.78 = (pred[8]{0:T(512)(128)(4,1)}, pred[8]{0:T(512)(128)(4,1)S(1)}, u32[]{:S(2)}) copy-start(pred[8]{0:T(512)(128)(4,1)S(1)} %get-tuple-element.258) | copy-start | bytes 28
  195.2 98.5 %copy-start.80 = (pred[8]{0:T(512)(128)(4,1)}, pred[8]{0:T(512)(128)(4,1)S(1)}, u32[]{:S(2)}) copy-start(pred[8]{0:T(512)(128)(4,1)S(1)} %get-tuple-element.259) | copy-start | bytes 28
  195.3 98.5 %copy-start.82 = (s32[8]{0:T(128)}, s32[8]{0:T(128)S(1)}, u32[]{:S(2)}) copy-start(s32[8]{0:T(128)S(1)} %get-tuple-element.260) | copy-start | bytes 100
  195.3 98.5 %copy-start.84 = (s32[8]{0:T(128)}, s32[8]{0:T(128)S(1)}, u32[]{:S(2)}) copy-start(s32[8]{0:T(128)S(1)} %get-tuple-element.261) | copy-start | bytes 100
  195.3 98.5 %copy-start.86 = (s32[8]{0:T(128)}, s32[8]{0:T(128)S(1)}, u32[]{:S(2)}) copy-start(s32[8]{0:T(128)S(1)} %get-tuple-element.262) | copy-start | bytes 100
  195.3 98.5 %copy-start.88 = (s32[8]{0:T(128)}, s32[8]{0:T(128)S(1)}, u32[]{:S(2)}) copy-start(s32[8]{0:T(128)S(1)} %get-tuple-element.263) | copy-start | bytes 100
  308.5 45.7 %all-to-all-start.3 = ((f32[16,1,32768]{2,1,0:T(1,128)}), f32[16,1,32768]{2,1,0:T(1,128)}, u32[]{:S(2)}, u32[]{:S(2)}) async-start(f32[16,1,32768]{2,1,0:T(1,128)} %copy.14), calls=%async_computation.3 | async-start | bytes 4194304 | tf_op jit(solution)/shard_map/all_to_all | solution.py:151
  354.3 52.5 %all-to-all-start.1 = ((f32[16,1,32768]{2,1,0:T(1,128)}), f32[16,1,32768]{2,1,0:T(1,128)}, u32[]{:S(2)}, u32[]{:S(2)}) async-start(f32[16,1,32768]{2,1,0:T(1,128)} %copy.12), calls=%async_computation.1 | async-start | bytes 4194304 | tf_op jit(solution)/shard_map/all_to_all | solution.py:150
  458.3 44.4 %collective-permute-start = (f32[524288]{0:T(1024)}, f32[524288]{0:T(1024)}, u32[]{:S(2)}, u32[]{:S(2)}) collective-permute-start(f32[524288]{0:T(1024)} %multiply_divide_fusion), channel_id=1, source_target_pairs={{0,16},{1,17},{2,18},{3,19},{4,20},{5,21},{6,22},{7,23},{8,24},{9,... | collective-permute-start | bytes 6291464 | tf_op jit(solution)/shard_map/ppermute | solution.py:14
  471.4 31.3 %copy-start.1 = (f32[1,524288]{1,0:T(1,128)S(1)}, f32[1,524288]{1,0:T(1,128)}, u32[]{:S(2)}) copy-start(f32[1,524288]{1,0:T(1,128)} %param.4) | copy-start | bytes 6291460
  (57 other events, 273.8 us)
where the time goes:
time: 551 us; the launch traced here: 543 us
  matrix products  128 us (23%)
  blocking collectives  112 us (20%)
  other arithmetic  79.7 us (14%)
  local copies, waits for them, and re-layouts  71.7 us (13%)
  waiting for transfers between devices  71.1 us (13%)
  between operations  45.2 us (8%)
  starting transfers between devices  34.8 us (6%)
    psum x2, blocking collectives, shards(): totals = lax.psum((jnp.sum(forward), jnp.sum(backward)), 'state')  79.9 us
    dot_general x10, matrix products, mix_local(): jnp.einsum('ij,ojk->oik', kron_matrix(thetas_local[offset:offset + width_...  58.3 us
    another operation x21, other arithmetic, bit_product(): pair = jnp.stack([anchor_zero[which], anchor_one[which]])  49.1 us
    dot_general x6, matrix products, mix_rows(): jnp.dot(kron_matrix(thetas_part), matrix, precision=lax.Precision.HIGHEST...  42.1 us
    all_to_all x2, waiting for transfers between devices, shards(): lax.all_to_all(fwd_part, 'state', split_axis=0, concat_axis=0, tiled=True)  34.4 us
    psum x1, blocking collectives, shards(): post_total = lax.psum(jnp.sum(product), 'state')  32.3 us
    dot_general x4, matrix products, mix_local(): jnp.dot(current, kron_matrix(thetas_local[:first_bits]), precision=lax.Pr...  27.7 us
    ppermute x1, waiting for transfers between devices, passed_along(): lax.ppermute(value, axis, [(source, source + steps) for source in range(f...  27.2 us
  transfers between devices with their start and end apart: 5, of which 4 were waited for; matrix products, arithmetic and copies ran while one was open for 26% of the time, Pallas kernels for 0%

commit v1 on v0

v1 whole, which is shorter than its diff:
```python
import functools

import jax
import jax.numpy as jnp
from jax import lax
from jax.experimental import pallas as pl
from jax.experimental.pallas import tpu as pltpu
from jax.sharding import PartitionSpec as P

PENALTY = 0.5
ERROR_RATE = 0.02
BASE_THETA = 0.01
LANES = 128
TILE = 8
MESH = pl.DeviceIdType.MESH
HIGHEST = lax.Precision.HIGHEST


def bits_of(size):
    return size.bit_length() - 1


def kernel(
    groups,
    segs,
    rows,
    masks,
    index,
    f_hbm,
    b_hbm,
    f_out,
    b_out,
    p_out,
    totals_out,
    f_in,
    b_in,
    f_send,
    f_mid,
    f_back,
    f_last,
    b_send,
    b_mid,
    b_back,
    b_last,
    f_raw,
    b_raw,
    p_raw,
    left,
    lane_mats,
    row_mats,
    tables,
    part_src,
    parts,
    load_sem,
    own_sem,
    out_sem,
    send_sem,
    recv_sem,
    seg_send,
    seg_recv,
    part_send,
    part_recv,
):
    me = lax.axis_index("state")
    seg = lax.axis_index("seg")
    later = lax.rem(seg + 1, segs)
    earlier = lax.rem(seg + segs - 1, segs)
    group_bits = bits_of(groups)
    lane_bits = bits_of(LANES)
    row_bits = bits_of(rows)
    swap_first = lane_bits + row_bits
    high_first = swap_first + group_bits
    half = rows // 2

    def partner(turn):
        odd = lax.rem(turn, 2)
        offset = (1 - odd) * (groups // 2 + lax.div(turn, 2)) + odd * lax.div(turn + 1, 2)
        other = 0
        for bit in range(group_bits):
            mine = lax.div(me, 2**bit)
            its = lax.div(offset, 2**bit)
            other = other + lax.rem(mine + its, 2) * 2**bit
        return other

    def each_partner(body):
        def step(turn, carry):
            body(partner(turn))
            return carry

        lax.fori_loop(0, groups - 1, step, 0)

    load_f = pltpu.make_async_copy(f_hbm, f_in, load_sem.at[0])
    load_b = pltpu.make_async_copy(b_hbm, b_in, load_sem.at[1])
    load_f.start()
    load_b.start()

    barrier = pltpu.get_barrier_semaphore()

    def greet(other):
        pl.semaphore_signal(barrier, inc=1, device_id={"state": other}, device_id_type=MESH)

    each_partner(greet)
    pl.semaphore_signal(barrier, inc=1, device_id={"seg": later}, device_id_type=MESH)
    pl.semaphore_signal(barrier, inc=1, device_id={"seg": earlier}, device_id_type=MESH)

    def theta(marker, bit):
        return lax.shift_left(jnp.int32(1), index[marker, bit]).astype(jnp.float32) * BASE_THETA

    def anchors(marker, bit):
        mask = masks[marker, bit]
        zero = jnp.where(lax.rem(mask, 2) == 1, 1.0, PENALTY).astype(jnp.float32)
        one = jnp.where(lax.div(mask, 2) == 1, 1.0, PENALTY).astype(jnp.float32)
        return zero, one

    def own_factor(marker, first):
        factor = jnp.float32(1.0)
        for bit in range(group_bits):
            zero, one = anchors(marker, first + bit)
            factor = factor * jnp.where(lax.rem(lax.div(me, 2**bit), 2) == 1, one, zero)
        return factor

    def group_factors(marker, first, own):
        factors = [own]
        for bit in range(group_bits):
            zero, one = anchors(marker, first + bit)
            factors = [f * zero for f in factors] + [f * one for f in factors]
        return factors

    def thetas(marker, first):
        return [theta(marker, first + bit) for bit in range(group_bits)]

    def mixed(values, mixing):
        values = list(values)
        for bit, amount in enumerate(mixing):
            for low in range(groups):
                high = low + 2**bit
                if low // 2**bit % 2 == 0:
                    moved = amount * (values[high] - values[low])
                    values[low] = values[low] + moved
                    values[high] = values[high] - moved
        return values

    def emitted(values, table, factors):
        return [
            v * (ERROR_RATE + (1.0 - ERROR_RATE) * (factor * table))
            for v, factor in zip(values, factors)
        ]

    def over_tiles(first, count, body, init):
        def step(which, carry):
            start = pl.multiple_of((first + which) * TILE, TILE)
            return body(pl.ds(start, TILE), carry)

        return lax.fori_loop(0, count, step, init)

    def loaded(ref, where):
        return [ref[group, where, :] for group in range(groups)]

    def stored(ref, where, values):
        for group in range(groups):
            ref[group, where, :] = values[group]

    def wave(number, source, target):
        where = pl.ds(number % 2 * half, half)

        def send(other):
            pltpu.make_async_remote_copy(
                src_ref=source.at[other, where],
                dst_ref=target.at[me, where],
                send_sem=send_sem.at[number],
                recv_sem=recv_sem.at[number],
                device_id={"state": other},
                device_id_type=MESH,
            ).start()

        each_partner(send)

    def wave_wait(number, ref, sems):
        view = ref.at[pl.ds(0, groups - 1), pl.ds(number % 2 * half, half)]
        pltpu.make_async_copy(view, view, sems.at[number]).wait()

    def own_copy(number, source, target):
        return pltpu.make_async_copy(source.at[me], target.at[me], own_sem.at[number])

    def share(which, partial):
        part_src[which] = partial
        parts[which, me] = partial

        def send(other):
            pltpu.make_async_remote_copy(
                src_ref=part_src.at[which],
                dst_ref=parts.at[which, me],
                send_sem=part_send.at[which],
                recv_sem=part_recv.at[which],
                device_id={"state": other},
                device_id_type=MESH,
            ).start()

        each_partner(send)

    def shared(which):
        view = parts.at[which, pl.ds(0, groups - 1)]
        pltpu.make_async_copy(view, view, part_send.at[which]).wait()
        pltpu.make_async_copy(view, view, part_recv.at[which]).wait()
        return jnp.sum(jnp.sum(parts[which], axis=0))

    def kron(marker, first, count):
        width = 2**count
        differs = lax.broadcasted_iota(jnp.int32, (width, width), 0) ^ lax.broadcasted_iota(
            jnp.int32, (width, width), 1
        )
        result = jnp.ones((width, width), jnp.float32)
        for bit in range(count):
            amount = theta(marker, first + bit)
            result = result * jnp.where((differs >> bit) & 1 == 0, 1.0 - amount, amount)
        return result

    def low_table(marker):
        lane = lax.broadcasted_iota(jnp.int32, (rows, LANES), 1)
        row = lax.broadcasted_iota(jnp.int32, (rows, LANES), 0)
        result = jnp.ones((rows, LANES), jnp.float32)
        for bit in range(swap_first):
            zero, one = anchors(marker, bit)
            spot = lane >> bit if bit < lane_bits else row >> (bit - lane_bits)
            result = result * jnp.where(spot & 1 == 1, one, zero)
        return result

    tiles = rows // TILE
    nothing = jnp.zeros((TILE, LANES), jnp.float32)

    load_f.wait()
    first_swap = thetas(0, swap_first)

    def start_forward(where, carry):
        stored(f_send, where, mixed(loaded(f_in, where), first_swap))
        return carry

    over_tiles(0, tiles, start_forward, 0)
    pl.semaphore_wait(barrier, groups + 1)
    wave(0, f_send, f_mid)
    wave(1, f_send, f_mid)
    own_f1 = own_copy(0, f_send, f_mid)
    own_f1.start()

    tables[1] = low_table(1)
    load_b.wait()
    last_swap = thetas(1, swap_first)
    last_factors = group_factors(1, swap_first, own_factor(1, high_first))

    def start_backward(where, carry):
        values = emitted(loaded(b_in, where), tables[1, where, :], last_factors)
        stored(b_send, where, mixed(values, last_swap))
        return carry

    over_tiles(0, tiles, start_backward, 0)
    own_b1 = own_copy(1, b_send, b_mid)
    own_b1.start()
    tables[0] = low_table(0)
    for marker in range(2):
        lane_mats[marker] = kron(marker, 0, lane_bits)
        row_mats[marker] = kron(marker, lane_bits, row_bits)
    high_mix = [thetas(0, high_first), thetas(1, high_first)]
    high_factors = group_factors(0, high_first, own_factor(0, swap_first))

    def low_mix(source, target, marker):
        def step(group, carry):
            part = jnp.dot(
                source[group],
                lane_mats[marker],
                precision=HIGHEST,
                preferred_element_type=jnp.float32,
            )
            target[group] = jnp.dot(
                row_mats[marker], part, precision=HIGHEST, preferred_element_type=jnp.float32
            )
            return carry

        lax.fori_loop(0, groups, step, 0)

    def middle(mid, back, before, after):
        low_mix(mid, mid, before)

        def step(where, total):
            values = mixed(loaded(mid, where), high_mix[before])
            values = emitted(values, tables[0, where, :], high_factors)
            stored(mid, where, mixed(values, high_mix[after]))
            return total + sum(values[1:], values[0])

        total = over_tiles(0, tiles, step, nothing)
        low_mix(mid, back, after)
        return total

    wave_wait(0, f_send, send_sem)
    wave(2, b_send, b_mid)
    wave_wait(1, f_send, send_sem)
    wave(3, b_send, b_mid)
    wave_wait(0, f_mid, recv_sem)
    wave_wait(1, f_mid, recv_sem)
    own_f1.wait()
    middle(f_mid, f_back, 0, 1)
    own_f2 = own_copy(2, f_back, f_last)
    own_f2.start()

    wave_wait(2, b_send, send_sem)
    wave(4, f_back, f_last)
    wave_wait(3, b_send, send_sem)
    wave(5, f_back, f_last)
    wave_wait(2, b_mid, recv_sem)
    wave_wait(3, b_mid, recv_sem)
    own_b1.wait()
    b_total = middle(b_mid, b_back, 1, 0)
    own_b2 = own_copy(3, b_back, b_last)
    own_b2.start()
    share(1, b_total)

    def to_later(part):
        where = pl.ds(part * half, half)
        return pltpu.make_async_remote_copy(
            src_ref=f_raw.at[:, where],
            dst_ref=left.at[:, where],
            send_sem=seg_send.at[part],
            recv_sem=seg_recv.at[part],
            device_id={"seg": later},
            device_id_type=MESH,
        )

    def finish_forward(where, total):
        values = emitted(
            mixed(loaded(f_last, where), last_swap), tables[1, where, :], last_factors
        )
        stored(f_raw, where, values)
        return total + sum(values[1:], values[0])

    def finish_backward(where, total):
        values = mixed(loaded(b_last, where), first_swap)
        stored(b_raw, where, values)
        for group in range(groups):
            beside = jnp.where(seg == 0, f_in[group, where, :], left[group, where, :])
            product = beside * values[group]
            p_raw[group, where, :] = product
            total = total + product
        return total

    own_f2.wait()
    f_total = nothing
    for part in range(2):
        wave_wait(4 + part, f_back, send_sem)
        wave(6 + part, b_back, b_last)
        wave_wait(4 + part, f_last, recv_sem)
        f_total = over_tiles(part * tiles // 2, tiles // 2, finish_forward, f_total)
        to_later(part).start()
    save_f = pltpu.make_async_copy(f_raw, f_out, out_sem.at[0])
    save_f.start()
    share(0, f_total)
    own_b2.wait()
    totals_out[0] = shared(0)
    totals_out[1] = shared(1)

    p_total = nothing
    saves = [save_f]
    for part in range(2):
        where = pl.ds(part * half, half)
        wave_wait(6 + part, b_last, recv_sem)
        to_later(part).wait_recv()
        p_total = over_tiles(part * tiles // 2, tiles // 2, finish_backward, p_total)
        for number, (source, target) in enumerate(((b_raw, b_out), (p_raw, p_out))):
            save = pltpu.make_async_copy(
                source.at[:, where], target.at[:, where], out_sem.at[1 + 2 * part + number]
            )
            if part == 0:
                save.start()
            saves.append(save)
    share(2, p_total)
    for save in saves[3:]:
        save.start()
    for part in range(2):
        wave_wait(6 + part, b_back, send_sem)
        to_later(part).wait_send()
    totals_out[2] = shared(2)
    for save in saves:
        save.wait()


def messages(groups, segs, forward, backward, masks, index):
    rows = forward.shape[0] // (groups * LANES)
    shape = (groups, rows, LANES)
    block = pltpu.VMEM(shape, jnp.float32)
    dma = pltpu.SemaphoreType.DMA
    whole = jax.ShapeDtypeStruct(shape, jnp.float32)
    anywhere = pl.BlockSpec(memory_space=pl.ANY)
    scalars = pl.BlockSpec(memory_space=pltpu.SMEM)
    size = forward.shape[0]
    return pl.pallas_call(
        functools.partial(kernel, groups, segs, rows),
        out_shape=(whole, whole, whole, jax.ShapeDtypeStruct((3,), jnp.float32)),
        in_specs=[scalars, scalars, anywhere, anywhere],
        out_specs=(anywhere, anywhere, anywhere, scalars),
        scratch_shapes=[block] * 14
        + [
            pltpu.VMEM((2, LANES, LANES), jnp.float32),
            pltpu.VMEM((2, rows, rows), jnp.float32),
            pltpu.VMEM((2, rows, LANES), jnp.float32),
            pltpu.VMEM((3, TILE, LANES), jnp.float32),
            pltpu.VMEM((3, groups, TILE, LANES), jnp.float32),
            dma((2,)),
            dma((4,)),
            dma((5,)),
            dma((8,)),
            dma((8,)),
            dma((2,)),
            dma((2,)),
            dma((3,)),
            dma((3,)),
        ],
        compiler_params=pltpu.CompilerParams(
            collective_id=0, has_side_effects=True, vmem_limit_bytes=44 * 1024 * 1024
        ),
        cost_estimate=pl.CostEstimate(
            flops=8 * size * (LANES + rows), bytes_accessed=20 * size, transcendentals=0
        ),
    )(masks, index, forward.reshape(shape), backward.reshape(shape))


def shards(forward_in, backward_in, compat_masks, theta_index):
    groups = lax.axis_size("state")
    segs = lax.axis_size("seg")
    total_states = forward_in.shape[1] * groups
    forward, backward, product, totals = messages(
        groups, segs, forward_in[0], backward_in[0], compat_masks, theta_index
    )
    means = totals / total_states
    outs = [
        (raw * (1.0 / means[which])).reshape(1, -1)
        for which, raw in enumerate((forward, backward, product))
    ]
    return (*outs, jnp.log(means[:2]).reshape(2, 1))


def solution(mesh):
    placed = (P("seg", "state"), P("seg", "state"), P("seg", None), P("seg", None))
    return jax.shard_map(
        shards,
        mesh=mesh,
        in_specs=placed,
        out_specs=(P("seg", "state"), P("seg", "state"), P("seg", "state"), P(None, "seg")),
        check_vma=False,
    )
```

time: 551 us -> 212 us (0.38); the launches traced: 543 us -> 212 us
  Pallas kernels: 0 us -> 201 us
  matrix products: 128 us -> 0 us
  blocking collectives: 112 us -> 0 us
  other arithmetic: 79.7 us -> 3.8 us
  waiting for transfers between devices: 71.1 us -> 0 us
  local copies, waits for them, and re-layouts: 71.7 us -> 4.05 us
  between operations: 45.2 us -> 2.73 us
  starting transfers between devices: 34.8 us -> 0 us
    pallas_call x0 -> x1, Pallas kernels: none -> 201 us  [messages(): pl.pallas_call(functools.partial(kernel, groups, segs, rows), out_shape=(...]
    dot_general x20 -> x0, matrix products: 128 us -> none  [the longest x10 58.3 us: mix_local(): jnp.einsum('ij,ojk->oik', kron_matrix(thetas_local[offset:offset + width_...]
    psum x3 -> x0, blocking collectives: 112 us -> none  [the longest x2 79.9 us: shards(): totals = lax.psum((jnp.sum(forward), jnp.sum(backward)), 'state')]
    another operation x21 -> x0, other arithmetic: 49.1 us -> none  [bit_product(): pair = jnp.stack([anchor_zero[which], anchor_one[which]])]
    all_to_all x4 -> x0, waiting for transfers between devices: 43.9 us -> none  [the longest x2 34.4 us: shards(): lax.all_to_all(fwd_part, 'state', split_axis=0, concat_axis=0, tiled=True)]
    all_to_all x4 -> x0, starting transfers between devices: 29.9 us -> none  [the longest x2 17.5 us: shards(): lax.all_to_all(fwd_part, 'state', split_axis=0, concat_axis=0, tiled=True)]
    ppermute x1 -> x0, waiting for transfers between devices: 27.2 us -> none  [passed_along(): lax.ppermute(value, axis, [(source, source + steps) for source in range(f...]
    unnamed x227 -> x6, local copies, waits for them, and re-layouts: 22.9 us -> 2.94 us
  transfers between devices with their start and end apart: 5 -> 0, of which waited for: 4 -> 0; matrix products, arithmetic and copies ran while one was open for 26% -> 0% of each run, Pallas kernels for 0% -> 0%
where the time goes in v1:
time: 212 us
  Pallas kernels  201 us (95%)
  local copies, waits for them, and re-layouts  4.05 us (2%)
  other arithmetic  3.8 us (2%)
  between operations  2.73 us (1%)
    pallas_call x1, Pallas kernels, messages(): pl.pallas_call(functools.partial(kernel, groups, segs, rows), out_shape=(...  201 us

profile of v1, /device:TPU:0, one launch (start us, length us, event | category | flops | bytes accessed | tf_op | source)
XLA Modules:
  0.0 211.8 jit_solution(10247908805387025766)
XLA Ops:
  0.6 0.0 copy-start
  0.6 1.6 copy-done
  2.2 0.0 copy-start.1
  2.2 0.7 copy-done.1
  2.9 0.0 copy-start.2
  2.9 0.7 copy-done.2
  3.6 201.2 %shard_map.75 = (f32[16,256,128]{2,1,0:T(8,128)S(1)}, f32[16,256,128]{2,1,0:T(8,128)S(1)}, f32[16,256,128]{2,1,0:T(8,128)S(1)}, f32[3]{0:T(128)S(1)}) custom-call(s32[2,23]{1,0:T(2,128)S(1)} %copy-done.1, s32[2,23]{1,0:T(2,128)S(1)} %copy-done.2, f32[16,256,128]{2,1,0:T(8,128)S(1)} %bitcast.10, f32[16,256,128]{2,1,0:T(8,128)} %bitcast.14), custom_call_target="tpu_custom_call" | custom-call | flops 1610612736 | bytes 10485760 | tf_op jit(solution)/shard_map/pallas_call | solution.py:393
  204.8 0.6 fusion
  206.1 1.5 broadcast_multiply_fusion.2
  209.0 2.3 %broadcast_multiply_fusion = (f32[16,256,128]{2,1,0:T(8,128)}, f32[16,256,128]{2,1,0:T(8,128)}) fusion(f32[16,256,128]{2,1,0:T(8,128)S(1)} %get-tuple-element.11, f32[]{:T(128)} %bitcast.6, f32[16,256,128]{2,1,0:T(8,128)S(1)} %get-tuple-element.10, f32[]{:T(128)} %bitcast.4), kind=kLoop, calls=%fused_computation | loop fusion | flops 1048576 | bytes 8388616 | tf_op jit(solution)/shard_map/mul | solution.py:433
  211.3 0.5 log_bitcast_fusion
  (1 shorter events, 0.0 us)
Async XLA Ops:
  0.6 1.6 copy-start
  2.2 0.7 copy-start.1
  2.9 0.7 copy-start.2

commit v2 on v1

--- a/solution.py
+++ b/solution.py
@@ -12,8 +12,9 @@
 BASE_THETA = 0.01
 LANES = 128
 TILE = 8
+CHUNKS = 4
+DEPTH = 2
 MESH = pl.DeviceIdType.MESH
-HIGHEST = lax.Precision.HIGHEST
 
 
 def bits_of(size):
@@ -24,14 +25,16 @@
     groups,
     segs,
     rows,
-    masks,
-    index,
+    masks_hbm,
+    index_hbm,
     f_hbm,
     b_hbm,
     f_out,
     b_out,
     p_out,
-    totals_out,
+    means_out,
+    masks,
+    index,
     f_in,
     b_in,
     f_send,
@@ -46,6 +49,7 @@
     b_raw,
     p_raw,
     left,
+    f_done,
     lane_mats,
     row_mats,
     tables,
@@ -70,7 +74,9 @@
     row_bits = bits_of(rows)
     swap_first = lane_bits + row_bits
     high_first = swap_first + group_bits
-    half = rows // 2
+    chunks = min(CHUNKS, rows // TILE)
+    part_rows = rows // chunks
+    total_states = groups * groups * rows * LANES
 
     def partner(turn):
         odd = lax.rem(turn, 2)
@@ -91,7 +97,11 @@
 
     load_f = pltpu.make_async_copy(f_hbm, f_in, load_sem.at[0])
     load_b = pltpu.make_async_copy(b_hbm, b_in, load_sem.at[1])
+    load_index = pltpu.make_async_copy(index_hbm, index, load_sem.at[2])
+    load_masks = pltpu.make_async_copy(masks_hbm, masks, load_sem.at[3])
+    load_index.start()
     load_f.start()
+    load_masks.start()
     load_b.start()
 
     barrier = pltpu.get_barrier_semaphore()
@@ -160,8 +170,26 @@
         for group in range(groups):
             ref[group, where, :] = values[group]
 
-    def wave(number, source, target):
-        where = pl.ds(number % 2 * half, half)
+    swaps = ((f_send, f_mid), (b_send, b_mid), (f_back, f_last), (b_back, b_last))
+
+    def wave_rows(number):
+        return pl.ds(number % chunks * part_rows, part_rows)
+
+    def wave_wait(number, side, sems):
+        view = swaps[number // chunks][side].at[pl.ds(0, groups - 1), wave_rows(number)]
+        pltpu.make_async_copy(view, view, sems.at[number]).wait()
+
+    def sent(number):
+        wave_wait(number, 0, send_sem)
+
+    def arrived(number):
+        wave_wait(number, 1, recv_sem)
+
+    def wave(number):
+        source, target = swaps[number // chunks]
+        where = wave_rows(number)
+        if number >= DEPTH:
+            sent(number - DEPTH)
 
         def send(other):
             pltpu.make_async_remote_copy(
@@ -175,10 +203,6 @@
 
         each_partner(send)
 
-    def wave_wait(number, ref, sems):
-        view = ref.at[pl.ds(0, groups - 1), pl.ds(number % 2 * half, half)]
-        pltpu.make_async_copy(view, view, sems.at[number]).wait()
-
     def own_copy(number, source, target):
         return pltpu.make_async_copy(source.at[me], target.at[me], own_sem.at[number])
 
@@ -202,7 +226,7 @@
         view = parts.at[which, pl.ds(0, groups - 1)]
         pltpu.make_async_copy(view, view, part_send.at[which]).wait()
         pltpu.make_async_copy(view, view, part_recv.at[which]).wait()
-        return jnp.sum(jnp.sum(parts[which], axis=0))
+        return jnp.sum(jnp.sum(parts[which], axis=0)) / total_states
 
     def kron(marker, first, count):
         width = 2**count
@@ -226,22 +250,27 @@
         return result
 
     tiles = rows // TILE
+    part_tiles = tiles // chunks
     nothing = jnp.zeros((TILE, LANES), jnp.float32)
 
+    load_index.wait()
+    first_swap = thetas(0, swap_first)
     load_f.wait()
-    first_swap = thetas(0, swap_first)
 
     def start_forward(where, carry):
         stored(f_send, where, mixed(loaded(f_in, where), first_swap))
         return carry
 
-    over_tiles(0, tiles, start_forward, 0)
-    pl.semaphore_wait(barrier, groups + 1)
-    wave(0, f_send, f_mid)
-    wave(1, f_send, f_mid)
+    for part in range(chunks):
+        over_tiles(part * part_tiles, part_tiles, start_forward, 0)
+        if part == 0:
+            pl.semaphore_wait(barrier, groups + 1)
+        if part < DEPTH:
+            wave(part)
     own_f1 = own_copy(0, f_send, f_mid)
     own_f1.start()
 
+    load_masks.wait()
     tables[1] = low_table(1)
     load_b.wait()
     last_swap = thetas(1, swap_first)
@@ -253,68 +282,80 @@
         return carry
 
     over_tiles(0, tiles, start_backward, 0)
+
+    def halves(value):
+        main = value.astype(jnp.bfloat16)
+        return main, (value - main.astype(jnp.float32)).astype(jnp.bfloat16)
+
+    def product(a, b):
+        return jnp.dot(a, b, preferred_element_type=jnp.float32)
+
+    for marker in range(2):
+        main, rest = halves(kron(marker, 0, lane_bits))
+        lane_mats[marker, :LANES] = main
+        lane_mats[marker, LANES : 2 * LANES] = main
+        lane_mats[marker, 2 * LANES :] = rest
+        main, rest = halves(kron(marker, lane_bits, row_bits))
+        row_mats[marker, 0] = main
+        row_mats[marker, 1] = rest
+
+    def low_mix(source, target, marker):
+        def step(pair, carry):
+            for which in range(2):
+                group = 2 * pair + which
+                main, rest = halves(source[group])
+                value = product(
+                    jnp.concatenate([main, rest], axis=1), lane_mats[marker, : 2 * LANES]
+                ) + product(main, lane_mats[marker, 2 * LANES :])
+                main, rest = halves(value)
+                both = product(row_mats[marker, 0], jnp.concatenate([main, rest], axis=1))
+                target[group] = (
+                    both[:, :LANES] + both[:, LANES:] + product(row_mats[marker, 1], main)
+                )
+            return carry
+
+        lax.fori_loop(0, groups // 2, step, 0)
+
+    low_mix(b_send, b_send, 1)
     own_b1 = own_copy(1, b_send, b_mid)
     own_b1.start()
     tables[0] = low_table(0)
-    for marker in range(2):
-        lane_mats[marker] = kron(marker, 0, lane_bits)
-        row_mats[marker] = kron(marker, lane_bits, row_bits)
     high_mix = [thetas(0, high_first), thetas(1, high_first)]
     high_factors = group_factors(0, high_first, own_factor(0, swap_first))
 
-    def low_mix(source, target, marker):
-        def step(group, carry):
-            part = jnp.dot(
-                source[group],
-                lane_mats[marker],
-                precision=HIGHEST,
-                preferred_element_type=jnp.float32,
-            )
-            target[group] = jnp.dot(
-                row_mats[marker], part, precision=HIGHEST, preferred_element_type=jnp.float32
-            )
-            return carry
-
-        lax.fori_loop(0, groups, step, 0)
-
-    def middle(mid, back, before, after):
-        low_mix(mid, mid, before)
-
+    def middle(mid, before, after):
         def step(where, total):
             values = mixed(loaded(mid, where), high_mix[before])
             values = emitted(values, tables[0, where, :], high_factors)
             stored(mid, where, mixed(values, high_mix[after]))
             return total + sum(values[1:], values[0])
 
-        total = over_tiles(0, tiles, step, nothing)
-        low_mix(mid, back, after)
-        return total
-
-    wave_wait(0, f_send, send_sem)
-    wave(2, b_send, b_mid)
-    wave_wait(1, f_send, send_sem)
-    wave(3, b_send, b_mid)
-    wave_wait(0, f_mid, recv_sem)
-    wave_wait(1, f_mid, recv_sem)
+        return over_tiles(0, tiles, step, nothing)
+
+    for number in range(DEPTH, chunks + DEPTH):
+        wave(number)
+    for number in range(chunks):
+        arrived(number)
     own_f1.wait()
-    middle(f_mid, f_back, 0, 1)
+    low_mix(f_mid, f_mid, 0)
+    middle(f_mid, 0, 1)
+    low_mix(f_mid, f_back, 1)
     own_f2 = own_copy(2, f_back, f_last)
     own_f2.start()
 
-    wave_wait(2, b_send, send_sem)
-    wave(4, f_back, f_last)
-    wave_wait(3, b_send, send_sem)
-    wave(5, f_back, f_last)
-    wave_wait(2, b_mid, recv_sem)
-    wave_wait(3, b_mid, recv_sem)
+    for number in range(chunks + DEPTH, 2 * chunks + DEPTH):
+        wave(number)
+    for number in range(chunks, 2 * chunks):
+        arrived(number)
     own_b1.wait()
-    b_total = middle(b_mid, b_back, 1, 0)
+    b_total = middle(b_mid, 1, 0)
+    low_mix(b_mid, b_back, 0)
     own_b2 = own_copy(3, b_back, b_last)
     own_b2.start()
     share(1, b_total)
 
     def to_later(part):
-        where = pl.ds(part * half, half)
+        where = pl.ds(part * part_rows, part_rows)
         return pltpu.make_async_remote_copy(
             src_ref=f_raw.at[:, where],
             dst_ref=left.at[:, where],
@@ -331,52 +372,100 @@
         stored(f_raw, where, values)
         return total + sum(values[1:], values[0])
 
+    own_f2.wait()
+    f_total = nothing
+    for part in range(chunks):
+        number = 2 * chunks + part
+        if number + DEPTH < 4 * chunks:
+            wave(number + DEPTH)
+        arrived(number)
+        f_total = over_tiles(part * part_tiles, part_tiles, finish_forward, f_total)
+        to_later(part).start()
+    share(0, f_total)
+    own_b2.wait()
+    means = [shared(0), shared(1)]
+    means_out[0] = means[0]
+    means_out[1] = means[1]
+    f_scale = jnp.float32(1.0) / means[0]
+    b_scale = jnp.float32(1.0) / means[1]
+
+    def scale_forward(where, carry):
+        stored(f_done, where, [value * f_scale for value in loaded(f_raw, where)])
+        return carry
+
     def finish_backward(where, total):
         values = mixed(loaded(b_last, where), first_swap)
-        stored(b_raw, where, values)
         for group in range(groups):
+            value = values[group] * b_scale
+            b_raw[group, where, :] = value
             beside = jnp.where(seg == 0, f_in[group, where, :], left[group, where, :])
-            product = beside * values[group]
-            p_raw[group, where, :] = product
-            total = total + product
+            joint = beside * value
+            p_raw[group, where, :] = joint
+            total = total + joint
         return total
 
-    own_f2.wait()
-    f_total = nothing
-    for part in range(2):
-        wave_wait(4 + part, f_back, send_sem)
-        wave(6 + part, b_back, b_last)
-        wave_wait(4 + part, f_last, recv_sem)
-        f_total = over_tiles(part * tiles // 2, tiles // 2, finish_forward, f_total)
-        to_later(part).start()
-    save_f = pltpu.make_async_copy(f_raw, f_out, out_sem.at[0])
-    save_f.start()
-    share(0, f_total)
-    own_b2.wait()
-    totals_out[0] = shared(0)
-    totals_out[1] = shared(1)
-
+    over_tiles(0, tiles, scale_forward, 0)
+    saves = [pltpu.make_async_copy(f_done, f_out, out_sem.at[0])]
+    saves[0].start()
     p_total = nothing
-    saves = [save_f]
-    for part in range(2):
-        where = pl.ds(part * half, half)
-        wave_wait(6 + part, b_last, recv_sem)
+    for part in range(chunks):
+        where = pl.ds(part * part_rows, part_rows)
+        number = 3 * chunks + part
+        if number + DEPTH < 4 * chunks:
+            wave(number + DEPTH)
+        arrived(number)
         to_later(part).wait_recv()
-        p_total = over_tiles(part * tiles // 2, tiles // 2, finish_backward, p_total)
-        for number, (source, target) in enumerate(((b_raw, b_out), (p_raw, p_out))):
+        p_total = over_tiles(part * part_tiles, part_tiles, finish_backward, p_total)
+        if part == chunks - 1:
+            share(2, p_total)
+        for side, (source, target) in enumerate(((b_raw, b_out), (p_raw, p_out))):
             save = pltpu.make_async_copy(
-                source.at[:, where], target.at[:, where], out_sem.at[1 + 2 * part + number]
+                source.at[:, where], target.at[:, where], out_sem.at[1 + 2 * part + side]
             )
-            if part == 0:
-                save.start()
+            save.start()
             saves.append(save)
-    share(2, p_total)
-    for save in saves[3:]:
+    for number in range(4 * chunks - DEPTH, 4 * chunks):
+        sent(number)
+    for part in range(chunks):
+        to_later(part).wait_send()
+    means_out[2] = shared(2)
+    for save in saves:
+        save.wait()
+
+
+def write_out(means, f_raw, b_raw, p_raw, f_out, b_out, p_out, logs_out, p_in, in_sem, out_sem):
+    rows = p_in.shape[1]
+    chunks = min(CHUNKS, rows // TILE)
+    part_rows = rows // chunks
+    views = [pl.ds(part * part_rows, part_rows) for part in range(chunks)]
+    reads = [
+        pltpu.make_async_copy(p_raw.at[:, where], p_in.at[:, where], in_sem.at[part])
+        for part, where in enumerate(views)
+    ]
+    for read in reads:
+        read.start()
+    saves = [
+        pltpu.make_async_copy(f_raw, f_out, out_sem.at[chunks]),
+        pltpu.make_async_copy(b_raw, b_out, out_sem.at[chunks + 1]),
+    ]
+    for save in saves:
         save.start()
-    for part in range(2):
-        wave_wait(6 + part, b_back, send_sem)
-        to_later(part).wait_send()
-    totals_out[2] = shared(2)
+    scale = jnp.float32(1.0) / means[2]
+    for part, where in enumerate(views):
+        reads[part].wait()
+
+        def step(tile, carry, part=part):
+            start = pl.multiple_of(part * part_rows + tile * TILE, TILE)
+            spot = pl.ds(start, TILE)
+            p_in[:, spot, :] = p_in[:, spot, :] * scale
+            return carry
+
+        lax.fori_loop(0, part_rows // TILE, step, 0)
+        save = pltpu.make_async_copy(p_in.at[:, where], p_out.at[:, where], out_sem.at[part])
+        save.start()
+        saves.append(save)
+    which = lax.broadcasted_iota(jnp.int32, (1, 2), 1)
+    logs_out[...] = jnp.log(jnp.where(which == 0, means[0], means[1]))
     for save in saves:
         save.wait()
 
@@ -384,31 +473,37 @@
 def messages(groups, segs, forward, backward, masks, index):
     rows = forward.shape[0] // (groups * LANES)
     shape = (groups, rows, LANES)
+    chunks = min(CHUNKS, rows // TILE)
     block = pltpu.VMEM(shape, jnp.float32)
     dma = pltpu.SemaphoreType.DMA
     whole = jax.ShapeDtypeStruct(shape, jnp.float32)
     anywhere = pl.BlockSpec(memory_space=pl.ANY)
     scalars = pl.BlockSpec(memory_space=pltpu.SMEM)
+    hbm = pl.BlockSpec(memory_space=pltpu.HBM)
     size = forward.shape[0]
-    return pl.pallas_call(
+    *raw, means = pl.pallas_call(
         functools.partial(kernel, groups, segs, rows),
         out_shape=(whole, whole, whole, jax.ShapeDtypeStruct((3,), jnp.float32)),
-        in_specs=[scalars, scalars, anywhere, anywhere],
+        in_specs=[hbm] * 4,
         out_specs=(anywhere, anywhere, anywhere, scalars),
-        scratch_shapes=[block] * 14
+        scratch_shapes=[
+            pltpu.SMEM(masks.shape, jnp.int32),
+            pltpu.SMEM(index.shape, jnp.int32),
+        ]
+        + [block] * 15
         + [
-            pltpu.VMEM((2, LANES, LANES), jnp.float32),
-            pltpu.VMEM((2, rows, rows), jnp.float32),
+            pltpu.VMEM((2, 3 * LANES, LANES), jnp.bfloat16),
+            pltpu.VMEM((2, 2, rows, rows), jnp.bfloat16),
             pltpu.VMEM((2, rows, LANES), jnp.float32),
             pltpu.VMEM((3, TILE, LANES), jnp.float32),
             pltpu.VMEM((3, groups, TILE, LANES), jnp.float32),
-            dma((2,)),
             dma((4,)),
-            dma((5,)),
-            dma((8,)),
-            dma((8,)),
-            dma((2,)),
-            dma((2,)),
+            dma((4,)),
+            dma((1 + 2 * chunks,)),
+            dma((4 * chunks,)),
+            dma((4 * chunks,)),
+            dma((chunks,)),
+            dma((chunks,)),
             dma((3,)),
             dma((3,)),
         ],
@@ -419,21 +514,22 @@
             flops=8 * size * (LANES + rows), bytes_accessed=20 * size, transcendentals=0
         ),
     )(masks, index, forward.reshape(shape), backward.reshape(shape))
+    *outs, logs = pl.pallas_call(
+        write_out,
+        out_shape=(whole, whole, whole, jax.ShapeDtypeStruct((1, 2), jnp.float32)),
+        in_specs=[scalars] + [anywhere] * 3,
+        out_specs=(hbm, hbm, hbm, pl.BlockSpec(memory_space=pltpu.VMEM)),
+        scratch_shapes=[block, dma((chunks,)), dma((chunks + 2,))],
+        compiler_params=pltpu.CompilerParams(vmem_limit_bytes=8 * 1024 * 1024),
+        cost_estimate=pl.CostEstimate(flops=size, bytes_accessed=24 * size, transcendentals=2),
+    )(means, *raw)
+    return (*(out.reshape(1, -1) for out in outs), logs.reshape(2, 1))
 
 
 def shards(forward_in, backward_in, compat_masks, theta_index):
     groups = lax.axis_size("state")
     segs = lax.axis_size("seg")
-    total_states = forward_in.shape[1] * groups
-    forward, backward, product, totals = messages(
-        groups, segs, forward_in[0], backward_in[0], compat_masks, theta_index
-    )
-    means = totals / total_states
-    outs = [
-        (raw * (1.0 / means[which])).reshape(1, -1)
-        for which, raw in enumerate((forward, backward, product))
-    ]
-    return (*outs, jnp.log(means[:2]).reshape(2, 1))
+    return messages(groups, segs, forward_in[0], backward_in[0], compat_masks, theta_index)
 
 
 def solution(mesh):

time: 212 us -> 210 us (level)
  Pallas kernels: 201 us -> 206 us
  other arithmetic: 3.8 us -> 0 us
    pallas_call x0 -> x1, Pallas kernels: none -> 3.93 us  [messages(): pl.pallas_call(write_out, out_shape=(whole, whole, whole, jax.ShapeDtypeS...]
    mul x2 -> x0, other arithmetic: 3.8 us -> none  [shards(): raw * (1.0 / means[which])]
where the time goes in v2:
time: 210 us; the launch traced here: 209 us
  Pallas kernels  206 us (98%)
  local copies, waits for them, and re-layouts  2.94 us (1%)
    pallas_call x1, Pallas kernels, messages(): pl.pallas_call(functools.partial(kernel, groups, segs, rows), out_shape=(...  202 us

profile of v2, /device:TPU:0, one launch (start us, length us, event | category | flops | bytes accessed | tf_op | source)
XLA Modules:
  0.0 209.5 jit_solution(12593808828947050959)
XLA Ops:
  0.6 0.0 copy-start
  0.6 1.6 copy-done
  2.2 0.0 copy-start.1
  2.2 0.7 copy-done.1
  2.9 0.0 copy-start.2
  2.9 0.7 copy-done.2
  3.6 201.9 %shard_map.75 = (f32[16,256,128]{2,1,0:T(8,128)S(1)}, f32[16,256,128]{2,1,0:T(8,128)S(1)}, f32[16,256,128]{2,1,0:T(8,128)S(1)}, f32[3]{0:T(128)S(1)}) custom-call(s32[2,23]{1,0:T(2,128)S(1)} %copy-done.1, s32[2,23]{1,0:T(2,128)S(1)} %copy-done.2, f32[16,256,128]{2,1,0:T(8,128)S(1)} %bitcast.6, f32[16,256,128]{2,1,0:T(8,128)} %bitcast.7), custom_call_target="tpu_custom_call" | custom-call | flops 1610612736 | bytes 10485760 | tf_op jit(solution)/shard_map/pallas_call | solution.py:484
  205.5 3.9 %shard_map.76 = (f32[16,256,128]{2,1,0:T(8,128)}, f32[16,256,128]{2,1,0:T(8,128)}, f32[16,256,128]{2,1,0:T(8,128)}, f32[1,2]{1,0:T(1,128)}) custom-call(f32[3]{0:T(128)S(1)} %get-tuple-element.12.means, f32[16,256,128]{2,1,0:T(8,128)S(1)} %get-tuple-element.13.f_raw, f32[16,256,128]{2,1,0:T(8,128)S(1)} %get-tuple-element.14.b_raw, ...), custom_call_target="tpu_custom_call" | custom-call | flops 524288 | bytes 12582912 | tf_op jit(solution)/shard_map/pallas_call | solution.py:517
Async XLA Ops:
  0.6 1.6 copy-start
  2.2 0.7 copy-start.1
  2.9 0.7 copy-start.2

commit v3 on v2

--- a/solution.py
+++ b/solution.py
@@ -13,7 +13,7 @@
 LANES = 128
 TILE = 8
 CHUNKS = 4
-DEPTH = 2
+DEPTH = 4
 MESH = pl.DeviceIdType.MESH
 
 
@@ -75,10 +75,14 @@
     swap_first = lane_bits + row_bits
     high_first = swap_first + group_bits
     chunks = min(CHUNKS, rows // TILE)
+    depth = min(DEPTH, chunks)
     part_rows = rows // chunks
     total_states = groups * groups * rows * LANES
 
-    def partner(turn):
+    first_turn = lax.rem(me * (groups // 2 - 1), groups - 1)
+
+    def partner(step):
+        turn = lax.rem(first_turn + step, groups - 1)
         odd = lax.rem(turn, 2)
         offset = (1 - odd) * (groups // 2 + lax.div(turn, 2)) + odd * lax.div(turn + 1, 2)
         other = 0
@@ -188,8 +192,8 @@
     def wave(number):
         source, target = swaps[number // chunks]
         where = wave_rows(number)
-        if number >= DEPTH:
-            sent(number - DEPTH)
+        if number >= depth:
+            sent(number - depth)
 
         def send(other):
             pltpu.make_async_remote_copy(
@@ -265,7 +269,7 @@
         over_tiles(part * part_tiles, part_tiles, start_forward, 0)
         if part == 0:
             pl.semaphore_wait(barrier, groups + 1)
-        if part < DEPTH:
+        if part < depth:
             wave(part)
     own_f1 = own_copy(0, f_send, f_mid)
     own_f1.start()
@@ -332,7 +336,7 @@
 
         return over_tiles(0, tiles, step, nothing)
 
-    for number in range(DEPTH, chunks + DEPTH):
+    for number in range(depth, chunks + depth):
         wave(number)
     for number in range(chunks):
         arrived(number)
@@ -343,7 +347,7 @@
     own_f2 = own_copy(2, f_back, f_last)
     own_f2.start()
 
-    for number in range(chunks + DEPTH, 2 * chunks + DEPTH):
+    for number in range(chunks + depth, 2 * chunks + depth):
         wave(number)
     for number in range(chunks, 2 * chunks):
         arrived(number)
@@ -376,8 +380,8 @@
     f_total = nothing
     for part in range(chunks):
         number = 2 * chunks + part
-        if number + DEPTH < 4 * chunks:
-            wave(number + DEPTH)
+        if number + depth < 4 * chunks:
+            wave(number + depth)
         arrived(number)
         f_total = over_tiles(part * part_tiles, part_tiles, finish_forward, f_total)
         to_later(part).start()
@@ -411,8 +415,8 @@
     for part in range(chunks):
         where = pl.ds(part * part_rows, part_rows)
         number = 3 * chunks + part
-        if number + DEPTH < 4 * chunks:
-            wave(number + DEPTH)
+        if number + depth < 4 * chunks:
+            wave(number + depth)
         arrived(number)
         to_later(part).wait_recv()
         p_total = over_tiles(part * part_tiles, part_tiles, finish_backward, p_total)
@@ -424,7 +428,7 @@
             )
             save.start()
             saves.append(save)
-    for number in range(4 * chunks - DEPTH, 4 * chunks):
+    for number in range(4 * chunks - depth, 4 * chunks):
         sent(number)
     for part in range(chunks):
         to_later(part).wait_send()

time: 210 us -> 207 us (0.986)
    pallas_call x1, Pallas kernels: 202 us -> 200 us  [messages(): pl.pallas_call(functools.partial(kernel, groups, segs, rows), out_shape=(...]
where the time goes in v3:
time: 207 us
  Pallas kernels  204 us (99%)
  local copies, waits for them, and re-layouts  2.94 us (1%)
    pallas_call x1, Pallas kernels, messages(): pl.pallas_call(functools.partial(kernel, groups, segs, rows), out_shape=(...  200 us

profile of v3, /device:TPU:0, one launch (start us, length us, event | category | flops | bytes accessed | tf_op | source)
XLA Modules:
  0.0 207.2 jit_solution(6481752511555624607)
XLA Ops:
  0.6 0.0 copy-start
  0.6 1.6 copy-done
  2.2 0.0 copy-start.1
  2.2 0.7 copy-done.1
  2.9 0.0 copy-start.2
  2.9 0.7 copy-done.2
  3.6 199.7 %shard_map.75 = (f32[16,256,128]{2,1,0:T(8,128)S(1)}, f32[16,256,128]{2,1,0:T(8,128)S(1)}, f32[16,256,128]{2,1,0:T(8,128)S(1)}, f32[3]{0:T(128)S(1)}) custom-call(s32[2,23]{1,0:T(2,128)S(1)} %copy-done.1, s32[2,23]{1,0:T(2,128)S(1)} %copy-done.2, f32[16,256,128]{2,1,0:T(8,128)S(1)} %bitcast.6, f32[16,256,128]{2,1,0:T(8,128)} %bitcast.7), custom_call_target="tpu_custom_call" | custom-call | flops 1610612736 | bytes 10485760 | tf_op jit(solution)/shard_map/pallas_call | solution.py:488
  203.3 3.9 %shard_map.76 = (f32[16,256,128]{2,1,0:T(8,128)}, f32[16,256,128]{2,1,0:T(8,128)}, f32[16,256,128]{2,1,0:T(8,128)}, f32[1,2]{1,0:T(1,128)}) custom-call(f32[3]{0:T(128)S(1)} %get-tuple-element.12.means, f32[16,256,128]{2,1,0:T(8,128)S(1)} %get-tuple-element.13.f_raw, f32[16,256,128]{2,1,0:T(8,128)S(1)} %get-tuple-element.14.b_raw, ...), custom_call_target="tpu_custom_call" | custom-call | flops 524288 | bytes 12582912 | tf_op jit(solution)/shard_map/pallas_call | solution.py:521
Async XLA Ops:
  0.6 1.6 copy-start
  2.2 0.7 copy-start.1
  2.9 0.7 copy-start.2

commit v4 on v3

--- a/solution.py
+++ b/solution.py
@@ -13,7 +13,7 @@
 LANES = 128
 TILE = 8
 CHUNKS = 4
-DEPTH = 4
+DEPTH = 3
 MESH = pl.DeviceIdType.MESH
 
 
@@ -186,14 +186,19 @@
     def sent(number):
         wave_wait(number, 0, send_sem)
 
+    here = set()
+
     def arrived(number):
-        wave_wait(number, 1, recv_sem)
+        if number not in here:
+            here.add(number)
+            wave_wait(number, 1, recv_sem)
 
     def wave(number):
         source, target = swaps[number // chunks]
         where = wave_rows(number)
         if number >= depth:
             sent(number - depth)
+            arrived(number - depth)
 
         def send(other):
             pltpu.make_async_remote_copy(

time: 207 us -> 208 us (level)
  no operation moved by 1% of the time
where the time goes in v4:
time: 208 us; the launch traced here: 207 us
  Pallas kernels  203 us (98%)
  local copies, waits for them, and re-layouts  2.94 us (1%)
    pallas_call x1, Pallas kernels, messages(): pl.pallas_call(functools.partial(kernel, groups, segs, rows), out_shape=(...  199 us

profile of v4, /device:TPU:0, one launch (start us, length us, event | category | flops | bytes accessed | tf_op | source)
XLA Modules:
  0.0 206.7 jit_solution(14790661422416798160)
XLA Ops:
  0.6 0.0 copy-start
  0.6 1.6 copy-done
  2.2 0.0 copy-start.1
  2.2 0.7 copy-done.1
  2.9 0.0 copy-start.2
  2.9 0.7 copy-done.2
  3.6 199.2 %shard_map.75 = (f32[16,256,128]{2,1,0:T(8,128)S(1)}, f32[16,256,128]{2,1,0:T(8,128)S(1)}, f32[16,256,128]{2,1,0:T(8,128)S(1)}, f32[3]{0:T(128)S(1)}) custom-call(s32[2,23]{1,0:T(2,128)S(1)} %copy-done.1, s32[2,23]{1,0:T(2,128)S(1)} %copy-done.2, f32[16,256,128]{2,1,0:T(8,128)S(1)} %bitcast.6, f32[16,256,128]{2,1,0:T(8,128)} %bitcast.7), custom_call_target="tpu_custom_call" | custom-call | flops 1610612736 | bytes 10485760 | tf_op jit(solution)/shard_map/pallas_call | solution.py:493
  202.8 3.9 %shard_map.76 = (f32[16,256,128]{2,1,0:T(8,128)}, f32[16,256,128]{2,1,0:T(8,128)}, f32[16,256,128]{2,1,0:T(8,128)}, f32[1,2]{1,0:T(1,128)}) custom-call(f32[3]{0:T(128)S(1)} %get-tuple-element.12.means, f32[16,256,128]{2,1,0:T(8,128)S(1)} %get-tuple-element.13.f_raw, f32[16,256,128]{2,1,0:T(8,128)S(1)} %get-tuple-element.14.b_raw, ...), custom_call_target="tpu_custom_call" | custom-call | flops 524288 | bytes 12582912 | tf_op jit(solution)/shard_map/pallas_call | solution.py:526
Async XLA Ops:
  0.6 1.6 copy-start
  2.2 0.7 copy-start.1
  2.9 0.7 copy-start.2

commit v5 on v3

--- a/solution.py
+++ b/solution.py
@@ -13,7 +13,7 @@
 LANES = 128
 TILE = 8
 CHUNKS = 4
-DEPTH = 4
+DEPTH = 3
 MESH = pl.DeviceIdType.MESH
 
 
@@ -50,6 +50,10 @@
     p_raw,
     left,
     f_done,
+    f_half,
+    b_half,
+    f_half2,
+    b_half2,
     lane_mats,
     row_mats,
     tables,
@@ -64,6 +68,9 @@
     seg_recv,
     part_send,
     part_recv,
+    near_send,
+    near_recv,
+    near_own,
 ):
     me = lax.axis_index("state")
     seg = lax.axis_index("seg")
@@ -79,6 +86,10 @@
     part_rows = rows // chunks
     total_states = groups * groups * rows * LANES
 
+    near = 2 ** (group_bits // 2)
+    far = groups // near
+    my_far = lax.div(me, near)
+    my_near = lax.rem(me, near)
     first_turn = lax.rem(me * (groups // 2 - 1), groups - 1)
 
     def partner(step):
@@ -174,41 +185,102 @@
         for group in range(groups):
             ref[group, where, :] = values[group]
 
-    swaps = ((f_send, f_mid), (b_send, b_mid), (f_back, f_last), (b_back, b_last))
+    swaps = (
+        (f_send, f_half, f_mid),
+        (b_send, b_half, b_mid),
+        (f_back, f_half2, f_last),
+        (b_back, b_half2, b_last),
+    )
+    own_copies = {}
+    planes = set()
+    here = set()
 
     def wave_rows(number):
         return pl.ds(number % chunks * part_rows, part_rows)
 
-    def wave_wait(number, side, sems):
-        view = swaps[number // chunks][side].at[pl.ds(0, groups - 1), wave_rows(number)]
+    def wave_wait(number, side, sems, blocks):
+        view = swaps[number // chunks][side].at[pl.ds(0, blocks), wave_rows(number)]
         pltpu.make_async_copy(view, view, sems.at[number]).wait()
 
+    far_blocks = (far - 1) * near
+    near_blocks = (near - 1) * far
+
     def sent(number):
-        wave_wait(number, 0, send_sem)
+        wave_wait(number, 0, send_sem, far_blocks)
+        wave_wait(number, 1, near_send, near_blocks)
+
+    def plane(number):
+        if number in planes:
+            return
+        planes.add(number)
+        swap = number // chunks
+        if swap in own_copies:
+            own_copies.pop(swap).wait()
+        source, target = swaps[swap][1:]
+        where = wave_rows(number)
+        wave_wait(number, 1, recv_sem, far_blocks)
+
+        def send(step, carry):
+            row = lax.div(step, near - 1)
+            other = lax.rem(my_near + 1 + lax.rem(step, near - 1), near)
+            pltpu.make_async_remote_copy(
+                src_ref=source.at[row * near + other, where],
+                dst_ref=target.at[row * near + my_near, where],
+                send_sem=near_send.at[number],
+                recv_sem=near_recv.at[number],
+                device_id={"state": my_far * near + other},
+                device_id_type=MESH,
+            ).start()
+            return carry
+
+        lax.fori_loop(0, near_blocks, send, 0)
+
+        def keep(row, carry):
+            spot = row * near + my_near
+            pltpu.make_async_copy(
+                source.at[spot, where], target.at[spot, where], near_own.at[number]
+            ).start()
+            return carry
+
+        lax.fori_loop(0, far, keep, 0)
 
     def arrived(number):
-        wave_wait(number, 1, recv_sem)
+        if number in here:
+            return
+        here.add(number)
+        plane(number)
+        wave_wait(number, 2, near_own, far)
+        wave_wait(number, 2, near_recv, near_blocks)
 
     def wave(number):
-        source, target = swaps[number // chunks]
+        source, target, _ = swaps[number // chunks]
         where = wave_rows(number)
         if number >= depth:
-            sent(number - depth)
-
-        def send(other):
+            plane(number - depth)
+        if number >= 2 * depth:
+            sent(number - 2 * depth)
+
+        def send(step, carry):
+            other = lax.rem(my_far + 1 + step, far)
             pltpu.make_async_remote_copy(
-                src_ref=source.at[other, where],
-                dst_ref=target.at[me, where],
+                src_ref=source.at[pl.ds(other * near, near), where],
+                dst_ref=target.at[pl.ds(my_far * near, near), where],
                 send_sem=send_sem.at[number],
                 recv_sem=recv_sem.at[number],
-                device_id={"state": other},
+                device_id={"state": other * near + my_near},
                 device_id_type=MESH,
             ).start()
-
-        each_partner(send)
-
-    def own_copy(number, source, target):
-        return pltpu.make_async_copy(source.at[me], target.at[me], own_sem.at[number])
+            return carry
+
+        lax.fori_loop(0, far - 1, send, 0)
+
+    def own_copy(swap):
+        where = pl.ds(my_far * near, near)
+        source, target, _ = swaps[swap]
+        own_copies[swap] = pltpu.make_async_copy(
+            source.at[where], target.at[where], own_sem.at[swap]
+        )
+        own_copies[swap].start()
 
     def share(which, partial):
         part_src[which] = partial
@@ -271,8 +343,7 @@
             pl.semaphore_wait(barrier, groups + 1)
         if part < depth:
             wave(part)
-    own_f1 = own_copy(0, f_send, f_mid)
-    own_f1.start()
+    own_copy(0)
 
     load_masks.wait()
     tables[1] = low_table(1)
@@ -321,8 +392,7 @@
         lax.fori_loop(0, groups // 2, step, 0)
 
     low_mix(b_send, b_send, 1)
-    own_b1 = own_copy(1, b_send, b_mid)
-    own_b1.start()
+    own_copy(1)
     tables[0] = low_table(0)
     high_mix = [thetas(0, high_first), thetas(1, high_first)]
     high_factors = group_factors(0, high_first, own_factor(0, swap_first))
@@ -340,22 +410,18 @@
         wave(number)
     for number in range(chunks):
         arrived(number)
-    own_f1.wait()
     low_mix(f_mid, f_mid, 0)
     middle(f_mid, 0, 1)
     low_mix(f_mid, f_back, 1)
-    own_f2 = own_copy(2, f_back, f_last)
-    own_f2.start()
+    own_copy(2)
 
     for number in range(chunks + depth, 2 * chunks + depth):
         wave(number)
     for number in range(chunks, 2 * chunks):
         arrived(number)
-    own_b1.wait()
     b_total = middle(b_mid, 1, 0)
     low_mix(b_mid, b_back, 0)
-    own_b2 = own_copy(3, b_back, b_last)
-    own_b2.start()
+    own_copy(3)
     share(1, b_total)
 
     def to_later(part):
@@ -376,7 +442,6 @@
         stored(f_raw, where, values)
         return total + sum(values[1:], values[0])
 
-    own_f2.wait()
     f_total = nothing
     for part in range(chunks):
         number = 2 * chunks + part
@@ -386,7 +451,6 @@
         f_total = over_tiles(part * part_tiles, part_tiles, finish_forward, f_total)
         to_later(part).start()
     share(0, f_total)
-    own_b2.wait()
     means = [shared(0), shared(1)]
     means_out[0] = means[0]
     means_out[1] = means[1]
@@ -428,7 +492,7 @@
             )
             save.start()
             saves.append(save)
-    for number in range(4 * chunks - depth, 4 * chunks):
+    for number in range(4 * chunks - 2 * depth, 4 * chunks):
         sent(number)
     for part in range(chunks):
         to_later(part).wait_send()
@@ -494,7 +558,7 @@
             pltpu.SMEM(masks.shape, jnp.int32),
             pltpu.SMEM(index.shape, jnp.int32),
         ]
-        + [block] * 15
+        + [block] * 19
         + [
             pltpu.VMEM((2, 3 * LANES, LANES), jnp.bfloat16),
             pltpu.VMEM((2, 2, rows, rows), jnp.bfloat16),
@@ -510,9 +574,12 @@
             dma((chunks,)),
             dma((3,)),
             dma((3,)),
+            dma((4 * chunks,)),
+            dma((4 * chunks,)),
+            dma((4 * chunks,)),
         ],
         compiler_params=pltpu.CompilerParams(
-            collective_id=0, has_side_effects=True, vmem_limit_bytes=44 * 1024 * 1024
+            collective_id=0, has_side_effects=True, vmem_limit_bytes=48 * 1024 * 1024
         ),
         cost_estimate=pl.CostEstimate(
             flops=8 * size * (LANES + rows), bytes_accessed=20 * size, transcendentals=0

time: 207 us -> 226 us (1.092)
  Pallas kernels: 204 us -> 222 us
    pallas_call x1, Pallas kernels: 200 us -> 218 us  [messages(): pl.pallas_call(functools.partial(kernel, groups, segs, rows), out_shape=(...]
where the time goes in v5:
time: 226 us
  Pallas kernels  222 us (98%)
  local copies, waits for them, and re-layouts  2.93 us (1%)
    pallas_call x1, Pallas kernels, messages(): pl.pallas_call(functools.partial(kernel, groups, segs, rows), out_shape=(...  218 us

profile of v5, /device:TPU:0, one launch (start us, length us, event | category | flops | bytes accessed | tf_op | source)
XLA Modules:
  0.0 225.5 jit_solution(14575598748440801094)
XLA Ops:
  0.6 0.0 copy-start.1
  0.6 0.7 copy-done.1
  1.3 0.0 copy-start.2
  1.3 0.7 copy-done.2
  2.0 218.0 %shard_map.75 = (f32[16,256,128]{2,1,0:T(8,128)S(1)}, f32[16,256,128]{2,1,0:T(8,128)S(1)}, f32[16,256,128]{2,1,0:T(8,128)}, f32[3]{0:T(128)S(1)}) custom-call(s32[2,23]{1,0:T(2,128)S(1)} %copy-done.1, s32[2,23]{1,0:T(2,128)S(1)} %copy-done.2, f32[16,256,128]{2,1,0:T(8,128)} %bitcast.6, f32[16,256,128]{2,1,0:T(8,128)} %bitcast.7), custom_call_target="tpu_custom_call" | custom-call | flops 1610612736 | bytes 10485760 | tf_op jit(solution)/shard_map/pallas_call | solution.py:552
  220.0 0.0 copy-start
  220.0 1.6 copy-done
  221.6 3.9 %shard_map.76 = (f32[16,256,128]{2,1,0:T(8,128)}, f32[16,256,128]{2,1,0:T(8,128)}, f32[16,256,128]{2,1,0:T(8,128)}, f32[1,2]{1,0:T(1,128)}) custom-call(f32[3]{0:T(128)S(1)} %get-tuple-element.12.means, f32[16,256,128]{2,1,0:T(8,128)S(1)} %get-tuple-element.13.f_raw, f32[16,256,128]{2,1,0:T(8,128)S(1)} %get-tuple-element.14.b_raw, f32[16,256,128]{2,1,0:T(8,128)S(1)} %copy-done), custom_call_target="tpu_custom_call" | custom-call | flops 524288 | bytes 12582912 | tf_op jit(solution)/shard_map/pallas_call | solution.py:588
Async XLA Ops:
  0.6 0.7 copy-start.1
  1.3 0.7 copy-start.2
  220.0 1.6 copy-start

commit v6 on v3

--- a/solution.py
+++ b/solution.py
@@ -360,14 +360,23 @@
 
     def to_later(part):
         where = pl.ds(part * part_rows, part_rows)
-        return pltpu.make_async_remote_copy(
-            src_ref=f_raw.at[:, where],
-            dst_ref=left.at[:, where],
-            send_sem=seg_send.at[part],
-            recv_sem=seg_recv.at[part],
-            device_id={"seg": later},
-            device_id_type=MESH,
-        )
+
+        def send(group, carry):
+            pltpu.make_async_remote_copy(
+                src_ref=f_raw.at[group, where],
+                dst_ref=left.at[group, where],
+                send_sem=seg_send.at[part],
+                recv_sem=seg_recv.at[part],
+                device_id={"seg": later},
+                device_id_type=MESH,
+            ).start()
+            return carry
+
+        lax.fori_loop(0, groups, send, 0)
+
+    def later_wait(part, sems):
+        view = left.at[:, pl.ds(part * part_rows, part_rows)]
+        pltpu.make_async_copy(view, view, sems.at[part]).wait()
 
     def finish_forward(where, total):
         values = emitted(
@@ -384,7 +393,7 @@
             wave(number + depth)
         arrived(number)
         f_total = over_tiles(part * part_tiles, part_tiles, finish_forward, f_total)
-        to_later(part).start()
+        to_later(part)
     share(0, f_total)
     own_b2.wait()
     means = [shared(0), shared(1)]
@@ -418,7 +427,7 @@
         if number + depth < 4 * chunks:
             wave(number + depth)
         arrived(number)
-        to_later(part).wait_recv()
+        later_wait(part, seg_recv)
         p_total = over_tiles(part * part_tiles, part_tiles, finish_backward, p_total)
         if part == chunks - 1:
             share(2, p_total)
@@ -431,7 +440,7 @@
     for number in range(4 * chunks - depth, 4 * chunks):
         sent(number)
     for part in range(chunks):
-        to_later(part).wait_send()
+        later_wait(part, seg_send)
     means_out[2] = shared(2)
     for save in saves:
         save.wait()

time: 207 us -> 207 us (level)
  no operation moved by 1% of the time
where the time goes in v6:
time: 207 us
  Pallas kernels  204 us (99%)
  local copies, waits for them, and re-layouts  2.94 us (1%)
    pallas_call x1, Pallas kernels, messages(): pl.pallas_call(functools.partial(kernel, groups, segs, rows), out_shape=(...  200 us

profile of v6, /device:TPU:0, one launch (start us, length us, event | category | flops | bytes accessed | tf_op | source)
XLA Modules:
  0.0 207.2 jit_solution(16765702294338046298)
XLA Ops:
  0.6 0.0 copy-start
  0.6 1.6 copy-done
  2.2 0.0 copy-start.1
  2.2 0.7 copy-done.1
  2.9 0.0 copy-start.2
  2.9 0.7 copy-done.2
  3.6 199.7 %shard_map.75 = (f32[16,256,128]{2,1,0:T(8,128)S(1)}, f32[16,256,128]{2,1,0:T(8,128)S(1)}, f32[16,256,128]{2,1,0:T(8,128)S(1)}, f32[3]{0:T(128)S(1)}) custom-call(s32[2,23]{1,0:T(2,128)S(1)} %copy-done.1, s32[2,23]{1,0:T(2,128)S(1)} %copy-done.2, f32[16,256,128]{2,1,0:T(8,128)S(1)} %bitcast.6, f32[16,256,128]{2,1,0:T(8,128)} %bitcast.7), custom_call_target="tpu_custom_call" | custom-call | flops 1610612736 | bytes 10485760 | tf_op jit(solution)/shard_map/pallas_call | solution.py:497
  203.3 3.9 %shard_map.76 = (f32[16,256,128]{2,1,0:T(8,128)}, f32[16,256,128]{2,1,0:T(8,128)}, f32[16,256,128]{2,1,0:T(8,128)}, f32[1,2]{1,0:T(1,128)}) custom-call(f32[3]{0:T(128)S(1)} %get-tuple-element.12.means, f32[16,256,128]{2,1,0:T(8,128)S(1)} %get-tuple-element.13.f_raw, f32[16,256,128]{2,1,0:T(8,128)S(1)} %get-tuple-element.14.b_raw, ...), custom_call_target="tpu_custom_call" | custom-call | flops 524288 | bytes 12582912 | tf_op jit(solution)/shard_map/pallas_call | solution.py:530
Async XLA Ops:
  0.6 1.6 copy-start
  2.2 0.7 copy-start.1
  2.9 0.7 copy-start.2
